TPU v7x, 128 devices: a whole 4x4x4 slice. The times are simulated.
128 devices in a mesh: patch: 64 (over x_lo, y, z, core), chan: 2 (over x_hi).
Axes of the slice: x: 4 (x_hi: 2, x_lo: 2; x = x_hi * 2 + x_lo), y: 4, z: 4, core: 2. Of those that a mesh axis runs over, the one named last changes fastest.
Arguments:
- features: bfloat16 [64, 524288], P('chan', 'patch'), may hold values from -6 to 6
- offsets: int32 [8, 524288], P(None, 'patch'), may hold values from -513 to 513, as said below
- edge_weights: float32 [8, 524288], P(None, 'patch'), may hold values from -1 to 0
- mix: bfloat16 [8, 64, 64], P(None, None, 'chan'), may hold values from -0.25 to 0.25
- bias: float32 [64], P('chan'), may hold values from -3 to 3
- owners: int32 [2048, 1], P('patch'), may hold values from 0 to 63; in each aligned block of 32 rows (0 to 31, 32 to 63, ...) at most 2 rows name the same one
Outputs:
- coarse: bfloat16 [64, 64, 2, 4096], P('patch', None, None, 'chan')
Inputs may be any that keep to these rules, and one draw needn't show every extreme that they name: `offsets`: A slot without a neighbour holds offset 0 and weight 0. `owners`: among the 32 blocks of one sub-patch no owner is named more than 2 times, a bound that some block reaches.
All inputs are finite; a program needn't handle non-finite values.
Results may differ from a plain program's by a relative error of at most 0.012.
Values may be sent and summed in bfloat16 or wider, within the bound.
A program may use at most 128 MiB of HBM per device.

v0:
```python
import jax
import jax.numpy as jnp
from jax import lax
from jax.sharding import PartitionSpec as P

K = 8
NBR = 8
HALO = 513


def padded_2(x, sides, width):
    for axis, dim in sides:
        size, length = (lax.axis_size(axis), x.shape[dim])
        up = [(i, (i + 1) % size) for i in range(size - 1)]
        down = [(j, i) for i, j in up]
        last = lax.slice_in_dim(x, length - width, length, axis=dim)
        first = lax.slice_in_dim(x, 0, width, axis=dim)
        before = lax.ppermute(last, axis, up)
        after = lax.ppermute(first, axis, down)
        x = jnp.concatenate([before, x, after], axis=dim)
    return x


def rim_patch(values):
    return padded_2(values.astype(jnp.bfloat16), (("patch", 1),), HALO).astype(values.dtype)


def neighbour_sum(values, offsets, edge_weights, spread):
    padded = spread(values)
    base = jnp.arange(values.shape[1], dtype=jnp.int32) + HALO
    total = jnp.zeros_like(values)
    for slot_index in range(NBR):
        picked = jnp.take(padded, base + offsets[slot_index], axis=1)
        total = total + edge_weights[slot_index][None, :] * picked
    return total


def chebyshev(start, offsets, edge_weights, spread, absorb, state):
    state = absorb(state, 0, start.astype(jnp.bfloat16))
    previous = start
    current = neighbour_sum(start, offsets, edge_weights, spread)
    state = absorb(state, 1, current.astype(jnp.bfloat16))
    for term_index in range(2, K):
        following = 2.0 * neighbour_sum(current, offsets, edge_weights, spread) - previous
        state = absorb(state, term_index, following.astype(jnp.bfloat16))
        previous, current = (current, following)
    return state


def pool_four(filtered):
    channels = filtered.shape[0]
    count = filtered.shape[1]
    return (
        filtered.astype(jnp.float32)
        .reshape(channels, count // 4, 4)
        .mean(axis=2)
        .astype(jnp.bfloat16)
    )


def add_rounded(parts, groups, shape):
    total = jnp.zeros(shape, jnp.float32)
    for group in range(groups):
        rounded = lax.optimization_barrier(parts[group].astype(jnp.bfloat16))
        total = total + rounded.astype(jnp.float32)
    return total


def body(features, offsets, edge_weights, mix, bias, owners):
    width = features.shape[0]
    pixels = features.shape[1]
    groups = lax.axis_size("chan")
    every = lax.all_gather(features, "chan", axis=0, tiled=True)
    weights_all = lax.all_gather(mix, "chan", axis=2, tiled=True)
    mine = lax.dynamic_slice_in_dim(weights_all, lax.axis_index("chan") * width, width, 1)

    def absorb_groups(parts, term_index, term_bf):
        return tuple(
            (
                parts[group]
                + jnp.dot(
                    mine[term_index][:, group * width : (group + 1) * width],
                    term_bf[group * width : (group + 1) * width],
                    preferred_element_type=jnp.float32,
                )
                for group in range(groups)
            )
        )

    empty = tuple((jnp.zeros((width, pixels), jnp.float32) for group in range(groups)))
    parts = chebyshev(
        every.astype(jnp.float32), offsets, edge_weights, rim_patch, absorb_groups, empty
    )
    total = add_rounded(parts, groups, (width, pixels))
    filtered = jax.nn.relu(total + bias[:, None]).astype(jnp.bfloat16)
    pooled = pool_four(filtered)
    nblocks = owners.shape[0]
    per_block = pixels // 4 // nblocks
    blocks = (
        pooled.reshape(width, nblocks, per_block)
        .transpose(1, 0, 2)
        .reshape(nblocks, width * per_block)
    )
    npatch = lax.axis_size("patch")
    dest = owners[:, 0]
    onehot = (dest[:, None] == jnp.arange(npatch, dtype=jnp.int32)[None, :]).astype(jnp.int32)
    ranks = jnp.cumsum(onehot, axis=0) - onehot
    slot = jnp.sum(ranks * onehot, axis=1)
    capacity = max(2, 2 * nblocks // npatch)
    outgoing = (
        jnp.zeros((npatch, capacity, width * per_block), jnp.bfloat16).at[dest, slot].set(blocks)
    )
    received = lax.all_to_all(outgoing, "patch", split_axis=0, concat_axis=0, tiled=True)
    return received[None]


def solution(mesh):
    return jax.shard_map(
        body,
        mesh=mesh,
        in_specs=(
            P("chan", "patch"),
            P(None, "patch"),
            P(None, "patch"),
            P(None, None, "chan"),
            P("chan"),
            P("patch", None),
        ),
        out_specs=P("patch", None, None, "chan"),
        check_vma=False,
    )
```

profile of v0, /device:TPU:1, one launch (start us, length us, event | category | flops | bytes accessed | tf_op | source)
XLA Modules:
  0.0 2199.6 jit_solution(60200730900735031)
XLA Ops:
  65.5 30.2 %gather_fusion.7 = f32[8192,64]{1,0:T(8,128)} fusion(f32[64,9218]{0,1:T(8,128)} %convert_element_type.80, s32[8192]{0:T(1024)S(1)} %fusion.91), kind=kCustom, calls=%fused_computation.7.clone | custom fusion | bytes 4227072 | tf_op jit(solution)/shard_map/jit(_take)/gather | solution.py:33
  126.0 30.3 %gather_fusion.5 = f32[8192,64]{1,0:T(8,128)} fusion(f32[64,9218]{0,1:T(8,128)} %convert_element_type.80, s32[8192]{0:T(1024)S(1)} %fusion.89), kind=kCustom, calls=%fused_computation.5.clone | custom fusion | bytes 4227072 | tf_op jit(solution)/shard_map/jit(_take)/gather | solution.py:33
  216.6 30.2 %gather_fusion.2 = f32[8192,64]{1,0:T(8,128)} fusion(f32[64,9218]{0,1:T(8,128)} %convert_element_type.80, s32[8192]{0:T(1024)S(1)} %fusion.86), kind=kCustom, calls=%fused_computation.2.clone | custom fusion | bytes 4227072 | tf_op jit(solution)/shard_map/jit(_take)/gather | solution.py:33
  277.1 30.4 %gather_fusion = f32[8192,64]{1,0:T(8,128)} fusion(f32[64,9218]{0,1:T(8,128)} %convert_element_type.80, s32[8192]{0:T(1024)S(1)} %fusion.84), kind=kCustom, calls=%fused_computation.clone | custom fusion | bytes 4227072 | tf_op jit(solution)/shard_map/jit(_take)/gather | solution.py:33
  356.0 30.2 %gather_fusion.15 = f32[8192,64]{1,0:T(8,128)} fusion(f32[64,9218]{0,1:T(8,128)} %convert_element_type.82, s32[8192]{0:T(1024)S(1)} %fusion.91), kind=kCustom, calls=%fused_computation.15.clone | custom fusion | bytes 4227072 | tf_op jit(solution)/shard_map/jit(_take)/gather | solution.py:33
  446.5 30.3 %gather_fusion.12 = f32[8192,64]{1,0:T(8,128)} fusion(f32[64,9218]{0,1:T(8,128)} %convert_element_type.82, s32[8192]{0:T(1024)S(1)} %fusion.88), kind=kCustom, calls=%fused_computation.12.clone | custom fusion | bytes 4227072 | tf_op jit(solution)/shard_map/jit(_take)/gather | solution.py:33
  537.2 30.2 %gather_fusion.9 = f32[8192,64]{1,0:T(8,128)} fusion(f32[64,9218]{0,1:T(8,128)} %convert_element_type.82, s32[8192]{0:T(1024)S(1)} %fusion.85), kind=kCustom, calls=%fused_computation.9.clone | custom fusion | bytes 4227072 | tf_op jit(solution)/shard_map/jit(_take)/gather | solution.py:33
  597.6 35.2 %fusion.117 = (bf16[64,8192]{0,1:T(8,128)(2,1)S(1)}, f32[64,8192]{0,1:T(8,128)}) fusion(bf16[64,8192]{0,1:T(8,128)(2,1)} %copy-done, f32[8192,64]{1,0:T(8,128)} %gather_fusion.15, pred[8192]{0:T(1024)(128)(4,1)} %get-tuple-element.54, f32[8192]{0:T(1024)} %bitcast.463, f32[8192,64]{1,0:T(8,128)} %gather_fusion.14, pred[8192]{0:T(1024)(128)(4,1)} %get-tuple-element.55, ...), kind=kLoop, calls=%fused_computation.275 | loop fusion | flops 14155776 | bytes 21299200 | tf_op jit(solution)/shard_map/convert_element_type | solution.py:45
  657.2 30.2 %gather_fusion.23 = f32[8192,64]{1,0:T(8,128)} fusion(f32[64,9218]{0,1:T(8,128)} %convert_element_type.85, s32[8192]{0:T(1024)S(1)} %fusion.91), kind=kCustom, calls=%fused_computation.23.clone | custom fusion | bytes 4227072 | tf_op jit(solution)/shard_map/jit(_take)/gather | solution.py:33
  717.6 30.3 %gather_fusion.21 = f32[8192,64]{1,0:T(8,128)} fusion(f32[64,9218]{0,1:T(8,128)} %convert_element_type.85, s32[8192]{0:T(1024)S(1)} %fusion.89), kind=kCustom, calls=%fused_computation.21.clone | custom fusion | bytes 4227072 | tf_op jit(solution)/shard_map/jit(_take)/gather | solution.py:33
  808.3 30.2 %gather_fusion.18 = f32[8192,64]{1,0:T(8,128)} fusion(f32[64,9218]{0,1:T(8,128)} %convert_element_type.85, s32[8192]{0:T(1024)S(1)} %fusion.86), kind=kCustom, calls=%fused_computation.18.clone | custom fusion | bytes 4227072 | tf_op jit(solution)/shard_map/jit(_take)/gather | solution.py:33
  868.7 30.3 %gather_fusion.16 = f32[8192,64]{1,0:T(8,128)} fusion(f32[64,9218]{0,1:T(8,128)} %convert_element_type.85, s32[8192]{0:T(1024)S(1)} %fusion.84), kind=kCustom, calls=%fused_computation.16.clone | custom fusion | bytes 4227072 | tf_op jit(solution)/shard_map/jit(_take)/gather | solution.py:33
  899.0 35.2 %fusion.115 = (bf16[64,8192]{0,1:T(8,128)(2,1)S(1)}, f32[64,8192]{0,1:T(8,128)}) fusion(f32[64,8192]{0,1:T(8,128)} %get-tuple-element.15, f32[8192,64]{1,0:T(8,128)} %gather_fusion.23, pred[8192]{0:T(1024)(128)(4,1)} %get-tuple-element.54, f32[8192]{0:T(1024)} %bitcast.464, f32[8192,64]{1,0:T(8,128)} %gather_fusion.22, ...), kind=kLoop, calls=%fused_computation.274 | loop fusion | flops 13631488 | bytes 22347776 | tf_op jit(solution)/shard_map/convert_element_type | solution.py:45
  959.2 30.2 %gather_fusion.31 = f32[8192,64]{1,0:T(8,128)} fusion(f32[64,9218]{0,1:T(8,128)} %convert_element_type.87, s32[8192]{0:T(1024)S(1)} %fusion.91), kind=kCustom, calls=%fused_computation.31.clone | custom fusion | bytes 4227072 | tf_op jit(solution)/shard_map/jit(_take)/gather | solution.py:33
  1019.6 30.3 %gather_fusion.29 = f32[8192,64]{1,0:T(8,128)} fusion(f32[64,9218]{0,1:T(8,128)} %convert_element_type.87, s32[8192]{0:T(1024)S(1)} %fusion.89), kind=kCustom, calls=%fused_computation.29.clone | custom fusion | bytes 4227072 | tf_op jit(solution)/shard_map/jit(_take)/gather | solution.py:33
  1110.3 30.2 %gather_fusion.26 = f32[8192,64]{1,0:T(8,128)} fusion(f32[64,9218]{0,1:T(8,128)} %convert_element_type.87, s32[8192]{0:T(1024)S(1)} %fusion.86), kind=kCustom, calls=%fused_computation.26.clone | custom fusion | bytes 4227072 | tf_op jit(solution)/shard_map/jit(_take)/gather | solution.py:33
  1170.8 30.4 %gather_fusion.24 = f32[8192,64]{1,0:T(8,128)} fusion(f32[64,9218]{0,1:T(8,128)} %convert_element_type.87, s32[8192]{0:T(1024)S(1)} %fusion.84), kind=kCustom, calls=%fused_computation.24.clone | custom fusion | bytes 4227072 | tf_op jit(solution)/shard_map/jit(_take)/gather | solution.py:33
  1255.3 30.2 %gather_fusion.39 = f32[8192,64]{1,0:T(8,128)} fusion(f32[64,9218]{0,1:T(8,128)} %convert_element_type.89, s32[8192]{0:T(1024)S(1)} %fusion.91), kind=kCustom, calls=%fused_computation.39.clone | custom fusion | bytes 4227072 | tf_op jit(solution)/shard_map/jit(_take)/gather | solution.py:33
  1315.7 30.3 %gather_fusion.37 = f32[8192,64]{1,0:T(8,128)} fusion(f32[64,9218]{0,1:T(8,128)} %convert_element_type.89, s32[8192]{0:T(1024)S(1)} %fusion.89), kind=kCustom, calls=%fused_computation.37.clone | custom fusion | bytes 4227072 | tf_op jit(solution)/shard_map/jit(_take)/gather | solution.py:33
  1406.4 30.2 %gather_fusion.34 = f32[8192,64]{1,0:T(8,128)} fusion(f32[64,9218]{0,1:T(8,128)} %convert_element_type.89, s32[8192]{0:T(1024)S(1)} %fusion.86), kind=kCustom, calls=%fused_computation.34.clone | custom fusion | bytes 4227072 | tf_op jit(solution)/shard_map/jit(_take)/gather | solution.py:33
  1466.8 30.3 %gather_fusion.32 = f32[8192,64]{1,0:T(8,128)} fusion(f32[64,9218]{0,1:T(8,128)} %convert_element_type.89, s32[8192]{0:T(1024)S(1)} %fusion.84), kind=kCustom, calls=%fused_computation.32.clone | custom fusion | bytes 4227072 | tf_op jit(solution)/shard_map/jit(_take)/gather | solution.py:33
  1497.1 35.3 %fusion.111 = (bf16[64,8192]{0,1:T(8,128)(2,1)S(1)}, f32[64,8192]{0,1:T(8,128)}) fusion(f32[64,8192]{0,1:T(8,128)} %get-tuple-element.11, f32[8192,64]{1,0:T(8,128)} %gather_fusion.39, pred[8192]{0:T(1024)(128)(4,1)} %get-tuple-element.54, f32[8192]{0:T(1024)} %bitcast.465, f32[8192,64]{1,0:T(8,128)} %gather_fusion.38, ...), kind=kLoop, calls=%fused_computation.272 | loop fusion | flops 13631488 | bytes 22347776 | tf_op jit(solution)/shard_map/convert_element_type | solution.py:45
  1587.5 30.3 %gather_fusion.46 = f32[8192,64]{1,0:T(8,128)} fusion(f32[64,9218]{0,1:T(8,128)} %convert_element_type.91, s32[8192]{0:T(1024)S(1)} %fusion.90), kind=kCustom, calls=%fused_computation.46.clone | custom fusion | bytes 4227072 | tf_op jit(solution)/shard_map/jit(_take)/gather | solution.py:33
  1678.2 30.2 %gather_fusion.43 = f32[8192,64]{1,0:T(8,128)} fusion(f32[64,9218]{0,1:T(8,128)} %convert_element_type.91, s32[8192]{0:T(1024)S(1)} %fusion.87), kind=kCustom, calls=%fused_computation.43.clone | custom fusion | bytes 4227072 | tf_op jit(solution)/shard_map/jit(_take)/gather | solution.py:33
  1738.6 30.3 %gather_fusion.41 = f32[8192,64]{1,0:T(8,128)} fusion(f32[64,9218]{0,1:T(8,128)} %convert_element_type.91, s32[8192]{0:T(1024)S(1)} %fusion.85), kind=kCustom, calls=%fused_computation.41.clone | custom fusion | bytes 4227072 | tf_op jit(solution)/shard_map/jit(_take)/gather | solution.py:33
  1769.0 30.3 %gather_fusion.40 = f32[8192,64]{1,0:T(8,128)} fusion(f32[64,9218]{0,1:T(8,128)} %convert_element_type.91, s32[8192]{0:T(1024)S(1)} %fusion.84), kind=kCustom, calls=%fused_computation.40.clone | custom fusion | bytes 4227072 | tf_op jit(solution)/shard_map/jit(_take)/gather | solution.py:33
  1852.3 30.2 %gather_fusion.55 = f32[8192,64]{1,0:T(8,128)} fusion(f32[64,9218]{0,1:T(8,128)} %convert_element_type.93, s32[8192]{0:T(1024)S(1)} %fusion.91), kind=kCustom, calls=%fused_computation.55.clone | custom fusion | bytes 4227072 | tf_op jit(solution)/shard_map/jit(_take)/gather | solution.py:33
  1882.5 30.3 %gather_fusion.54 = f32[8192,64]{1,0:T(8,128)} fusion(f32[64,9218]{0,1:T(8,128)} %convert_element_type.93, s32[8192]{0:T(1024)S(1)} %fusion.90), kind=kCustom, calls=%fused_computation.54.clone | custom fusion | bytes 4227072 | tf_op jit(solution)/shard_map/jit(_take)/gather | solution.py:33
  2003.4 30.3 %gather_fusion.50 = f32[8192,64]{1,0:T(8,128)} fusion(f32[64,9218]{0,1:T(8,128)} %convert_element_type.93, s32[8192]{0:T(1024)S(1)} %fusion.86), kind=kCustom, calls=%fused_computation.50.clone | custom fusion | bytes 4227072 | tf_op jit(solution)/shard_map/jit(_take)/gather | solution.py:33
  2033.6 30.2 %gather_fusion.49 = f32[8192,64]{1,0:T(8,128)} fusion(f32[64,9218]{0,1:T(8,128)} %convert_element_type.93, s32[8192]{0:T(1024)S(1)} %fusion.85), kind=kCustom, calls=%fused_computation.49.clone | custom fusion | bytes 4227072 | tf_op jit(solution)/shard_map/jit(_take)/gather | solution.py:33
  2063.9 30.3 %gather_fusion.48 = f32[8192,64]{1,0:T(8,128)} fusion(f32[64,9218]{0,1:T(8,128)} %convert_element_type.93, s32[8192]{0:T(1024)S(1)} %fusion.84), kind=kCustom, calls=%fused_computation.48.clone | custom fusion | bytes 4227072 | tf_op jit(solution)/shard_map/jit(_take)/gather | solution.py:33
  2142.3 49.7 %all_to_all.5 = bf16[64,2,2048]{2,1,0:T(2,128)(2,1)S(1)} all-to-all(bf16[64,2,2048]{2,1,0:T(2,128)(2,1)S(1)} %scatter_fusion), channel_id=1, replica_groups=mesh['patch'=64,'chan'=2] {'patch'}, dimensions={0} | all-to-all | bytes 1048576 | tf_op jit(solution)/shard_map/all_to_all | solution.py:113
  (254 shorter events, 1182.4 us)
Async XLA Ops:
  6.5 31.0 %all-gather.2.cloned.1.call-start = ((), (), s32[]{:S(2)}) async-start(), calls=%async_computation.1 | async-start | bytes 1572864 | tf_op jit(solution)/shard_map/all_gather | solution.py:73
  39.8 10.1 collective-permute-start.1
  42.4 7.5 collective-permute-start
  277.1 30.4 %copy-start.29 = (pred[8192]{0:T(1024)(128)(4,1)S(1)}, pred[8192]{0:T(1024)(128)(4,1)}, u32[]{:S(2)}) copy-start(pred[8192]{0:T(1024)(128)(4,1)} %get-tuple-element.60) | copy-start | bytes 24580
  277.1 30.4 %copy-start.33 = (pred[8192]{0:T(1024)(128)(4,1)S(1)}, pred[8192]{0:T(1024)(128)(4,1)}, u32[]{:S(2)}) copy-start(pred[8192]{0:T(1024)(128)(4,1)} %get-tuple-element.61) | copy-start | bytes 24580
  277.1 30.4 %copy-start.37 = (pred[8192]{0:T(1024)(128)(4,1)S(1)}, pred[8192]{0:T(1024)(128)(4,1)}, u32[]{:S(2)}) copy-start(pred[8192]{0:T(1024)(128)(4,1)} %get-tuple-element.58) | copy-start | bytes 24580
  277.1 30.4 %copy-start.41 = (pred[8192]{0:T(1024)(128)(4,1)S(1)}, pred[8192]{0:T(1024)(128)(4,1)}, u32[]{:S(2)}) copy-start(pred[8192]{0:T(1024)(128)(4,1)} %get-tuple-element.59) | copy-start | bytes 24580
  277.1 30.4 %copy-start.45 = (pred[8192]{0:T(1024)(128)(4,1)S(1)}, pred[8192]{0:T(1024)(128)(4,1)}, u32[]{:S(2)}) copy-start(pred[8192]{0:T(1024)(128)(4,1)} %get-tuple-element.54) | copy-start | bytes 24580
  277.1 30.4 %copy-start.49 = (pred[8192]{0:T(1024)(128)(4,1)S(1)}, pred[8192]{0:T(1024)(128)(4,1)}, u32[]{:S(2)}) copy-start(pred[8192]{0:T(1024)(128)(4,1)} %get-tuple-element.55) | copy-start | bytes 24580
  331.8 8.5 collective-permute-start.3
  333.8 6.4 collective-permute-start.2
  597.6 41.2 %copy-start.58 = (bf16[32,64]{0,1:T(8,128)(2,1)S(1)}, bf16[32,64]{0,1:T(8,128)(2,1)}, u32[]{:S(2)}) copy-start(bf16[32,64]{0,1:T(8,128)(2,1)} %get-tuple-element.51) | copy-start | bytes 12292
  632.9 8.6 collective-permute-start.5
  635.0 6.5 collective-permute-start.4
  899.0 40.9 %copy-start.7 = (f32[32,8192]{1,0:T(8,128)S(1)}, f32[32,8192]{1,0:T(8,128)}, u32[]{:S(2)}) copy-start(f32[32,8192]{1,0:T(8,128)} %convolution_add_fusion.5) | copy-start | bytes 3145732
  899.0 40.9 %copy-start.57 = (bf16[32,64]{0,1:T(8,128)(2,1)S(1)}, bf16[32,64]{0,1:T(8,128)(2,1)}, u32[]{:S(2)}) copy-start(bf16[32,64]{0,1:T(8,128)(2,1)} %get-tuple-element.50) | copy-start | bytes 12292
  934.3 9.3 collective-permute-start.7
  936.2 7.3 collective-permute-start.6
  1170.7 30.4 %copy-start.30 = (pred[8192]{0:T(1024)(128)(4,1)S(1)}, pred[8192]{0:T(1024)(128)(4,1)}, u32[]{:S(2)}) copy-start(pred[8192]{0:T(1024)(128)(4,1)} %get-tuple-element.60) | copy-start | bytes 24580
  1170.7 30.4 %copy-start.34 = (pred[8192]{0:T(1024)(128)(4,1)S(1)}, pred[8192]{0:T(1024)(128)(4,1)}, u32[]{:S(2)}) copy-start(pred[8192]{0:T(1024)(128)(4,1)} %get-tuple-element.61) | copy-start | bytes 24580
  1201.2 35.6 %copy-start.8 = (f32[32,8192]{1,0:T(8,128)S(1)}, f32[32,8192]{1,0:T(8,128)}, u32[]{:S(2)}) copy-start(f32[32,8192]{1,0:T(8,128)} %convolution_add_fusion.4) | copy-start | bytes 3145732
  1201.3 35.6 %copy-start.56 = (bf16[32,64]{0,1:T(8,128)(2,1)S(1)}, bf16[32,64]{0,1:T(8,128)(2,1)}, u32[]{:S(2)}) copy-start(bf16[32,64]{0,1:T(8,128)(2,1)} %get-tuple-element.49) | copy-start | bytes 12292
  1231.1 8.4 collective-permute-start.9
  1233.2 6.4 collective-permute-start.8
  1497.1 40.9 %copy-start.9 = (f32[32,8192]{1,0:T(8,128)S(1)}, f32[32,8192]{1,0:T(8,128)}, u32[]{:S(2)}) copy-start(f32[32,8192]{1,0:T(8,128)} %convolution_add_fusion.3) | copy-start | bytes 3145732
  1497.1 40.9 %copy-start.55 = (bf16[32,64]{0,1:T(8,128)(2,1)S(1)}, bf16[32,64]{0,1:T(8,128)(2,1)}, u32[]{:S(2)}) copy-start(bf16[32,64]{0,1:T(8,128)(2,1)} %get-tuple-element.48) | copy-start | bytes 12292
  1532.4 9.3 collective-permute-start.11
  1534.3 7.3 collective-permute-start.10
  1799.4 34.5 %copy-start.11 = (f32[32,8192]{1,0:T(8,128)S(1)}, f32[32,8192]{1,0:T(8,128)}, u32[]{:S(2)}) copy-start(f32[32,8192]{1,0:T(8,128)} %convolution_add_fusion.2) | copy-start | bytes 3145732
  1799.4 34.5 %copy-start.54 = (bf16[32,64]{0,1:T(8,128)(2,1)S(1)}, bf16[32,64]{0,1:T(8,128)(2,1)}, u32[]{:S(2)}) copy-start(bf16[32,64]{0,1:T(8,128)(2,1)} %get-tuple-element.47) | copy-start | bytes 12292
  1827.9 8.7 collective-permute-start.13
  1830.0 6.6 collective-permute-start.12
  (44 other events, 1165.2 us)
Sparse Core Ops, SparseCore 0:
  9.0 28.5 all-gather.1
where the time goes:
time: 2210 us; the launch traced here: 2200 us
  local copies, waits for them, and re-layouts  1790 us (81%)
  other arithmetic  257 us (12%)
  blocking collectives  55.8 us (3%)
  starting transfers between devices  40 us (2%)
  matrix products  24.3 us (1%)
    gather x56, local copies, waits for them, and re-layouts, neighbour_sum(): picked = jnp.take(padded, base + offsets[slot_index], axis=1)  1690 us
    convert_element_type x6, other arithmetic, chebyshev(): state = absorb(state, term_index, following.astype(jnp.bfloat16))  192 us
    concatenate x7, local copies, waits for them, and re-layouts, padded_2(): x = jnp.concatenate([before, x, after], axis=dim)  84.7 us
    all_to_all x1, blocking collectives, body(): lax.all_to_all(outgoing, 'patch', split_axis=0, concat_axis=0, tiled=True)  49.7 us
  transfers between devices with their start and end apart: 15, of which 1 were waited for; matrix products, arithmetic and copies ran while one was open for 2% of the time, Pallas kernels for 0%

commit v1 on v0

v1 whole, which is shorter than its diff:
```python
import functools

import jax
import jax.numpy as jnp
from jax import lax
from jax.experimental import pallas as pl
from jax.experimental.pallas import tpu as pltpu
from jax.sharding import PartitionSpec as P

MESH = pl.DeviceIdType.MESH
BF = jnp.bfloat16
F32 = jnp.float32
K = 8
CH = 64
OWN = 16
EXT = 7
NB = OWN + EXT
HALO = 640
LANES = HALO + NB * 256 + HALO
OUT_W = EXT * 256 + HALO
WIN = 1280
NPX = NB * 256
S3 = 1152
S4 = 1664


def place(line):
    n, q = line // 4, line % 4
    return 2 * n + q % 2, (q // 2 + n % 2) % 2


def iota(shape, dim):
    return lax.broadcasted_iota(jnp.int32, shape, dim)


def cheb_kernel(np_, feat, offs, wts, mix, bias, own_ref, out_ref,
                tb, fp, wm, ot, wt, cor, s16, w16, x3, mixall, biasall, inv, inv_s,
                msg, snd, t0_s, t0_r, tab_l, tab_s, tab_r, par_s, par_r,
                in_s, in_r, mid_s, mid_r, sw_s, sw_r, loc):
    p = lax.axis_index("patch")
    g = lax.axis_index("chan")
    n, c = p // 2, p % 2
    gx = (g + n) % 2
    line = 4 * n + 2 * gx + c
    last = 2 * np_ - 1
    sib = (p + 1 - 2 * c, g)
    partner = (p, 1 - g)
    first_core = c == 0
    home = gx == c
    ng = np_ // 2

    outer = pl.multiple_of((1 - c) * 0 + c * (LANES - OUT_W), 128)
    for k in range(1, K - 1):
        tb[k, :, pl.ds(outer, OUT_W)] = jnp.zeros((CH, OUT_W), BF)
    at_end = (line == 0) | (line == last)

    @pl.when(at_end)
    def _():
        tb[0, :, pl.ds(outer, OUT_W)] = jnp.zeros((CH, OUT_W), BF)
        to = pl.multiple_of(c * OWN * 256, 128)
        ot[:, pl.ds(to, EXT * 256)] = jnp.zeros((8, EXT * 256), jnp.int32)
        wt[:, pl.ds(to, EXT * 256)] = jnp.zeros((8, EXT * 256), F32)

    msg[2 * OWN] = jnp.zeros((16, 128), BF)

    bar = pltpu.get_barrier_semaphore()
    for dn in (-1, 0, 1):
        for dc in (0, 1):
            for dg in (0, 1):
                pp = 2 * (n + dn) + dc

                @pl.when((n + dn >= 0) & (n + dn < ng) & ~((pp == p) & (dg == g)))
                def _():
                    pl.semaphore_signal(bar, inc=1, device_id=(pp, dg), device_id_type=MESH)
    pl.semaphore_wait(bar, 11 - 4 * jnp.where((n == 0) | (n == ng - 1), 1, 0))

    half = 4096
    main_dst = pl.multiple_of((1 - c) * EXT * 256, 128)
    ext_dst = pl.multiple_of(c * OWN * 256, 128)
    sib_dst = pl.multiple_of(c * EXT * 256, 128)

    def tables(fn):
        fn(0, offs, ot)
        fn(1, wts, wt)

    def tab_main_local(i, src, dst):
        return pltpu.make_async_copy(src.at[:, pl.ds(pl.multiple_of(c * half, 128), half)],
                                     dst.at[:, pl.ds(main_dst, half)], tab_l.at[i])

    def tab_main_remote(i, src, dst):
        return pltpu.make_async_remote_copy(
            src_ref=src.at[:, pl.ds(pl.multiple_of((1 - c) * half, 128), half)],
            dst_ref=dst.at[:, pl.ds(sib_dst, half)],
            send_sem=tab_s.at[i], recv_sem=tab_r.at[i], device_id=sib, device_id_type=MESH)

    def tab_ext_local(i, src, dst):
        return pltpu.make_async_copy(
            src.at[:, pl.ds(pl.multiple_of((1 - c) * (8192 - EXT * 256), 128), EXT * 256)],
            dst.at[:, pl.ds(ext_dst, EXT * 256)], tab_l.at[i])

    out_line = line - 1 + 2 * c
    outp, outg = place(out_line)
    has_out = ~at_end
    other_ext = pl.multiple_of((1 - c) * OWN * 256, 128)

    def tab_ext_remote(i, src, dst):
        return pltpu.make_async_remote_copy(
            src_ref=src.at[:, pl.ds(pl.multiple_of(c * (8192 - EXT * 256), 128), EXT * 256)],
            dst_ref=dst.at[:, pl.ds(other_ext, EXT * 256)],
            send_sem=tab_s.at[2 + i], recv_sem=tab_r.at[2 + i],
            device_id=(outp, outg), device_id_type=MESH)

    @pl.when(home)
    def _():
        tables(lambda i, s, d: tab_main_local(i, s, d).start())
        tables(lambda i, s, d: tab_main_remote(i, s, d).start())

    @pl.when(~home)
    def _():
        tables(lambda i, s, d: tab_ext_local(i, s, d).start())

    row = pl.multiple_of(32 * g, 32)
    flows = (
        (2 * p, 0, HALO + 4096, LANES - HALO - 4096, 0),
        (2 * p + 1, 4096 - HALO, HALO + 4096, 0, 0),
        (2 * p - 1, 0, OUT_W, LANES - OUT_W, 2),
        (2 * p + 2, 8192 - OUT_W, OUT_W, 0, 2),
    )

    def flow_parts(i):
        target, src0, size, dst0, sem = flows[i]
        src = feat.at[:, pl.ds(src0, size)]
        dst = tb.at[0, pl.ds(row, 32), pl.ds(dst0, size)]
        return target, src, dst, sem + g

    def flow_ok(i):
        target = flows[i][0]
        return (target >= 0) & (target <= last)

    def flow_remote(i):
        target, src, dst, sem = flow_parts(i)
        tp, tg = place(target)
        return pltpu.make_async_remote_copy(
            src_ref=src, dst_ref=dst, send_sem=t0_s.at[i], recv_sem=t0_r.at[sem],
            device_id=(tp, tg), device_id_type=MESH)

    for i in range(4):
        target, src, dst, sem = flow_parts(i)

        @pl.when(flow_ok(i) & (target == line))
        def _():
            pltpu.make_async_copy(src, dst, t0_r.at[sem]).start()

        @pl.when(flow_ok(i) & (target != line))
        def _():
            flow_remote(i).start()

    @pl.when(home & has_out)
    def _():
        tables(lambda i, s, d: tab_ext_remote(i, s, d).start())

    mixcat = jnp.concatenate([mix[k] for k in range(K)], axis=0)
    oi, oo = iota((64, 64), 0), iota((64, 64), 1)
    wanted = (oi // 16 % 2) * 32 + 2 * (oi % 16) + oi // 32
    perm = jnp.where(oo == wanted, 1.0, 0.0).astype(BF)
    mixall[g] = lax.dot_general(perm, mixcat, (((1,), (1,)), ((), ())),
                                preferred_element_type=F32).astype(BF)
    biasall[g] = jnp.zeros((8, 128), F32)
    biasall[g, 0:1, 0:32] = bias[...]

    rowv = jnp.broadcast_to(own_ref[...], (32, 32))
    si, sl = iota((32, 32), 0), iota((32, 32), 1)
    bi, bl = iota((32, 128), 0), iota((32, 128), 1)
    col = jnp.sum(jnp.where(si == sl, rowv, 0), axis=1, keepdims=True)
    same = (jnp.broadcast_to(col, (32, 32)) == rowv) & (sl < si)
    slot = jnp.sum(jnp.where(same, 1, 0), axis=1, keepdims=True)
    key = col * 2 + slot
    hit = jnp.sum(jnp.where(jnp.broadcast_to(key, (32, 128)) == bl, bi + 1, 0), axis=0, keepdims=True)
    inv[c] = jnp.broadcast_to(jnp.where(hit == 0, 2 * OWN, hit - 1), (8, 128))

    par = [
        pltpu.make_async_remote_copy(src_ref=mixall.at[g], dst_ref=mixall.at[g], send_sem=par_s.at[0],
                                     recv_sem=par_r.at[0], device_id=partner, device_id_type=MESH),
        pltpu.make_async_remote_copy(src_ref=biasall.at[g], dst_ref=biasall.at[g], send_sem=par_s.at[1],
                                     recv_sem=par_r.at[1], device_id=partner, device_id_type=MESH),
        pltpu.make_async_remote_copy(src_ref=inv.at[c], dst_ref=inv.at[c], send_sem=par_s.at[2],
                                     recv_sem=par_r.at[2], device_id=sib, device_id_type=MESH),
    ]
    for cp in par:
        cp.start()

    def block_of(i):
        return c * i + (1 - c) * (NB - 1 - i)

    base = [(iota((16, 256), 0) + 16 * r).astype(jnp.int16) for r in range(16)]

    def build(i, carry):
        b = block_of(i)
        lanes = pl.ds(pl.multiple_of(256 * b, 256), 256)
        s = iota((8, 256), 1) + ot[:, lanes] + 512
        w = wt[:, lanes]
        cl = jnp.sum(jnp.where(s == -1, w, 0.0), axis=0, keepdims=True)
        cr = jnp.sum(jnp.where(s == WIN, w, 0.0), axis=0, keepdims=True)
        cor[b, 0:1, :] = cl
        cor[b, 1:2, :] = cr
        full = w
        for r in range(1, 8):
            full = full + jnp.where(s == pltpu.roll(s, r, 0), pltpu.roll(w, r, 0), 0.0)
        for j in range(8):
            s16[j] = jnp.broadcast_to(s[j:j + 1], (16, 256)).astype(jnp.int16)
            w16[j] = jnp.broadcast_to(full[j:j + 1], (16, 256)).astype(BF)
        for q in range(WIN // 256):
            acc = [jnp.zeros((16, 256), BF)] * 16
            for j in range(8):
                sq = s16[j] - jnp.int16(256 * q)
                wq = w16[j]
                acc = [jnp.where(base[r] == sq, wq, acc[r]) for r in range(16)]
            for r in range(16):
                wm[b, 256 * q + 16 * r:256 * q + 16 * (r + 1), :] = acc[r]
        return carry

    lo1 = jnp.where(home, 0, OWN)
    hi1 = jnp.where(home, OWN, NB)
    lo2 = jnp.where(home, OWN, 0)
    hi2 = jnp.where(home, NB, OWN)

    @pl.when(home)
    def _():
        tables(lambda i, s, d: tab_main_local(i, s, d).wait())

    @pl.when(~home)
    def _():
        tables(lambda i, s, d: tab_ext_local(i, s, d).wait())

    lax.fori_loop(lo1, hi1, build, 0)

    @pl.when(~home)
    def _():
        tables(lambda i, s, d: pltpu.make_async_copy(
            s.at[:, pl.ds(0, half)], d.at[:, pl.ds(main_dst, half)], tab_r.at[i]).wait())

    @pl.when(home & has_out)
    def _():
        tables(lambda i, s, d: pltpu.make_async_copy(
            s.at[:, pl.ds(0, EXT * 256)], d.at[:, pl.ds(ext_dst, EXT * 256)], tab_r.at[2 + i]).wait())

    lax.fori_loop(lo2, hi2, build, 0)

    main_at = pl.multiple_of((1 - c) * (LANES - HALO - 4096), 128)
    for gg in range(2):
        pltpu.make_async_copy(feat.at[:, pl.ds(0, HALO + 4096)],
                              tb.at[0, pl.ds(32 * gg, 32), pl.ds(main_at, HALO + 4096)],
                              t0_r.at[gg]).wait()

        @pl.when(has_out)
        def _():
            pltpu.make_async_copy(feat.at[:, pl.ds(0, OUT_W)],
                                  tb.at[0, pl.ds(32 * gg, 32), pl.ds(outer, OUT_W)],
                                  t0_r.at[2 + gg]).wait()

    def block(k, i):
        b = block_of(i)
        at = pl.multiple_of(256 * b, 256)
        win = tb[k - 1, :, pl.ds(at + 128, WIN)]
        u = jnp.dot(win, wm[b], preferred_element_type=F32)
        left = pltpu.roll(tb[k - 1, :, pl.ds(at, 128)].astype(F32), 1, 1)
        right = pltpu.roll(tb[k - 1, :, pl.ds(at + 1408, 128)].astype(F32), 127, 1)
        u = u + jnp.concatenate([left * cor[b, 0:1, 0:128], right * cor[b, 1:2, 128:256]], axis=1)
        if k == 1:
            t = u
        elif k == 2:
            t = 2.0 * u - tb[0, :, pl.ds(at + HALO, 256)].astype(F32)
        else:
            t = 2.0 * u - fp[k % 2, :, pl.ds(at, 256)]
        if k < K - 1:
            fp[k % 2, :, pl.ds(at, 256)] = t
        tb[k, :, pl.ds(at + HALO, 256)] = t.astype(BF)

    def run(k, lo, hi, group=4):
        full = (hi - lo) // group

        def some(m, carry):
            for r in range(group):
                block(k, lo + m * group + r)
            return carry

        if full > 1:
            lax.fori_loop(0, full, some, 0)
            lo = lo + full * group
        for i in range(lo, hi):
            block(k, i)

    own_at = HALO + (1 - c) * EXT * 256
    edge_src = pl.multiple_of(own_at + (1 - c) * (4096 - HALO), 128)
    edge_dst = pl.multiple_of(c * (LANES - HALO), 128)

    def inner(k):
        return pltpu.make_async_remote_copy(
            src_ref=tb.at[k, :, pl.ds(edge_src, HALO)], dst_ref=tb.at[k, :, pl.ds(edge_dst, HALO)],
            send_sem=in_s.at[k], recv_sem=in_r.at[k], device_id=sib, device_id_type=MESH)

    def outer_copy(k, width, m):
        src = pl.multiple_of(own_at + c * (4096 - width), 128)
        if k == 3:
            dst = x3.at[:, :]
        else:
            dst = tb.at[k, :, pl.ds(pl.multiple_of((1 - c) * (LANES - OUT_W) + c * (OUT_W - width), 128), width)]
        return pltpu.make_async_remote_copy(
            src_ref=tb.at[k, :, pl.ds(src, width)], dst_ref=dst,
            send_sem=mid_s.at[m], recv_sem=mid_r.at[m], device_id=(outp, outg), device_id_type=MESH)

    run(1, 0, 3)
    inner(1).start()
    run(1, 3, 23)
    inner(1).wait_recv()
    run(2, 0, 3)
    inner(2).start()
    run(2, 3, 21)
    inner(2).wait_recv()
    run(3, 0, 3)
    inner(3).start()
    run(3, 3, 19)

    @pl.when(has_out)
    def _():
        outer_copy(3, S3, 0).start()

    inner(3).wait_recv()
    run(4, 9, 16)

    @pl.when(has_out)
    def _():
        outer_copy(4, S4, 1).start()

    run(4, 0, 3)
    inner(4).start()
    run(4, 3, 9)
    inner(4).wait_recv()
    run(5, 0, 3)
    inner(5).start()
    run(5, 3, 13)

    @pl.when(has_out)
    def _():
        outer_copy(3, S3, 0).wait_recv()
        outer_copy(4, S4, 1).wait_recv()
        d3 = pl.multiple_of((1 - c) * (EXT * 256 - S3) + c * OWN * 256, 128)
        fp[1, :, pl.ds(d3, S3)] = x3[...].astype(F32)
        d4 = pl.multiple_of((1 - c) * (EXT * 256 - 768) + c * OWN * 256, 128)
        fp[0, :, pl.ds(d4, 768)] = tb[4, :, pl.ds(d4 + HALO, 768)].astype(F32)

    run(5, 13, 21)
    inner(5).wait_recv()
    run(6, 0, 3)
    inner(6).start()
    run(6, 3, 19)
    inner(6).wait_recv()
    run(7, 0, 16)

    pltpu.make_async_copy(mixall.at[1 - g], mixall.at[1 - g], par_r.at[0]).wait()
    pltpu.make_async_copy(biasall.at[1 - g], biasall.at[1 - g], par_r.at[1]).wait()
    pltpu.make_async_copy(inv.at[1 - c], inv.at[1 - c], par_r.at[2]).wait()
    to_smem = pltpu.make_async_copy(inv.at[gx], inv_s, loc.at[0])
    to_smem.start()
    o1, l1 = iota((64, 128), 0), iota((64, 128), 1)
    brow = jnp.where(o1 // 16 % 2 == 0, biasall[0, 0:1, :], biasall[1, 0:1, :])
    bcol = jnp.sum(jnp.where(l1 == 2 * (o1 % 16) + o1 // 32, brow, 0.0), axis=1, keepdims=True)
    pi, pq = iota((512, 128), 0), iota((512, 128), 1)
    pool = jnp.where(pi % 256 // 4 + 64 * (pi // 256) == pq, 0.25, 0.0).astype(BF)

    def finish(b, carry):
        at = pl.multiple_of(own_at + 256 * b, 128)
        total = bcol
        for gg in range(2):
            rhs = jnp.concatenate([tb[k, 32 * gg:32 * gg + 32, pl.ds(at, 256)] for k in range(K)], axis=0)
            part = jnp.dot(mixall[gg], rhs, preferred_element_type=F32)
            total = total + part.astype(BF).astype(F32)
        filt = jnp.maximum(total, 0.0).astype(BF)
        lhs = jnp.concatenate([filt[0:32], filt[32:64]], axis=1)
        pooled = jnp.dot(lhs, pool, preferred_element_type=F32).astype(BF)
        sel = jnp.where(c == 0, pooled[0:16].astype(F32), pooled[16:32].astype(F32)).astype(BF)
        oth = jnp.where(c == 0, pooled[16:32].astype(F32), pooled[0:16].astype(F32)).astype(BF)
        msg[c * OWN + b] = sel
        snd[b] = oth
        return carry

    def swap(m):
        part = pl.ds(pl.multiple_of(8 * m, 8), 8)
        return pltpu.make_async_remote_copy(
            src_ref=snd.at[part], dst_ref=msg.at[pl.ds(c * OWN + 8 * m, 8)],
            send_sem=sw_s.at[m], recv_sem=sw_r.at[m], device_id=sib, device_id_type=MESH)

    for m in range(2):
        for r in range(8):
            finish(8 * m + r, 0)
        swap(m).start()
    to_smem.wait()
    for m in range(2):
        pltpu.make_async_copy(msg.at[pl.ds((1 - c) * OWN + 8 * m, 8)],
                              msg.at[pl.ds((1 - c) * OWN + 8 * m, 8)], sw_r.at[m]).wait()

    ei, ej = iota((32, 32), 0), iota((32, 32), 1)
    weave = jnp.where(ej == (ei % 2) * 16 + ei // 2, 1.0, 0.0).astype(BF)

    def assemble(m, carry):
        cols = []
        for r in range(4):
            o = 4 * m + r
            cols.append(jnp.concatenate([msg[inv_s[0, 2 * o]], msg[inv_s[0, 2 * o + 1]]], axis=0))
        res = jnp.dot(weave, jnp.concatenate(cols, axis=1), preferred_element_type=F32).astype(BF)
        for r in range(4):
            out_ref[4 * m + r] = res[:, 128 * r:128 * (r + 1)]
        return carry

    lax.fori_loop(0, np_ // 4, assemble, 0)

    @pl.when(home)
    def _():
        tables(lambda i, s, d: tab_main_remote(i, s, d).wait_send())

    @pl.when(home & has_out)
    def _():
        tables(lambda i, s, d: tab_ext_remote(i, s, d).wait_send())

    for i in range(4):
        @pl.when(flow_ok(i) & (flows[i][0] != line))
        def _():
            flow_remote(i).wait_send()

    for cp in par:
        cp.wait_send()
    for k in range(1, K - 1):
        inner(k).wait_send()

    @pl.when(has_out)
    def _():
        outer_copy(3, S3, 0).wait_send()
        outer_copy(4, S4, 1).wait_send()

    for m in range(2):
        swap(m).wait_send()


def dispatch_kernel(np_, out_ref, got_ref, ss, rs):
    p = lax.axis_index("patch")
    g = lax.axis_index("chan")
    n, c = p // 2, p % 2
    src = 2 * n + (g + n) % 2
    bar = pltpu.get_barrier_semaphore()

    def hello(i, carry):
        j = (i + p) % np_
        pp = 2 * (j // 2) + g
        gg = j % 2

        @pl.when(~((pp == p) & (gg == g)))
        def _():
            pl.semaphore_signal(bar, inc=1, device_id=(pp, gg), device_id_type=MESH)
        return carry

    lax.fori_loop(0, np_, hello, 0)
    pl.semaphore_wait(bar, np_ - jnp.where(c == g, 1, 0))

    def copy(o):
        return pltpu.make_async_remote_copy(
            src_ref=out_ref.at[o], dst_ref=got_ref.at[src], send_sem=ss.at[o], recv_sem=rs.at[src],
            device_id=(o, c), device_id_type=MESH)

    def send(i, carry):
        o = (p + i) % np_
        me = (o == p) & (c == g)

        @pl.when(me)
        def _():
            pltpu.make_async_copy(out_ref.at[o], got_ref.at[src], rs.at[src]).start()

        @pl.when(~me)
        def _():
            copy(o).start()
        return carry

    lax.fori_loop(0, np_, send, 0)

    def take(i, carry):
        pltpu.make_async_copy(got_ref.at[i], got_ref.at[i], rs.at[i]).wait()
        return carry

    lax.fori_loop(0, np_, take, 0)

    def sent(o, carry):
        @pl.when(~((o == p) & (c == g)))
        def _():
            copy(o).wait_send()
        return carry

    lax.fori_loop(0, np_, sent, 0)


def body(features, offsets, edge_weights, mix, bias, owners):
    np_ = lax.axis_size("patch")
    any_, vmem = pl.BlockSpec(memory_space=pl.ANY), pl.BlockSpec(memory_space=pltpu.VMEM)
    dma, vm = pltpu.SemaphoreType.DMA, pltpu.VMEM
    out = pl.pallas_call(
        functools.partial(cheb_kernel, np_),
        out_shape=jax.ShapeDtypeStruct((np_, 32, 128), BF),
        in_specs=[any_, any_, any_, vmem, vmem, vmem],
        out_specs=vmem,
        scratch_shapes=[
            vm((K, CH, LANES), BF), vm((2, CH, NPX), F32), vm((NB, WIN, 256), BF),
            vm((8, NPX), jnp.int32), vm((8, NPX), F32), vm((NB, 8, 256), F32),
            vm((8, 16, 256), jnp.int16), vm((8, 16, 256), BF), vm((CH, S3), BF),
            vm((2, 64, 256), BF), vm((2, 8, 128), F32), vm((2, 8, 128), jnp.int32),
            pltpu.SMEM((8, 128), jnp.int32),
            vm((2 * OWN + 1, 16, 128), BF), vm((OWN, 16, 128), BF),
            dma((4,)), dma((4,)), dma((2,)), dma((4,)), dma((4,)), dma((3,)), dma((3,)),
            dma((K,)), dma((K,)), dma((2,)), dma((2,)), dma((2,)), dma((2,)), dma((1,)),
        ],
        compiler_params=pltpu.CompilerParams(
            vmem_limit_bytes=62 << 20, collective_id=0, has_side_effects=True),
        name="cheb",
    )(features, offsets, edge_weights, mix.transpose(0, 2, 1), bias.reshape(1, -1), owners.reshape(1, -1))
    got = pl.pallas_call(
        functools.partial(dispatch_kernel, np_),
        out_shape=jax.ShapeDtypeStruct((np_, 32, 128), BF),
        in_specs=[any_],
        out_specs=any_,
        scratch_shapes=[dma((np_,)), dma((np_,))],
        compiler_params=pltpu.CompilerParams(
            vmem_limit_bytes=62 << 20, collective_id=1, has_side_effects=True),
        name="dispatch",
    )(out)
    got = got.reshape(np_, 16, 2, 128).transpose(0, 2, 1, 3).reshape(np_, 2, 2048)
    return got[None]


def solution(mesh):
    return jax.shard_map(
        body,
        mesh=mesh,
        in_specs=(
            P("chan", "patch"),
            P(None, "patch"),
            P(None, "patch"),
            P(None, None, "chan"),
            P("chan"),
            P("patch", None),
        ),
        out_specs=P("patch", None, None, "chan"),
        check_vma=False,
    )
```

time: 2210 us -> 92.1 us (0.04)
  local copies, waits for them, and re-layouts: 1790 us -> 2.2 us
  other arithmetic: 257 us -> 0 us
  Pallas kernels: 0 us -> 89.7 us
  blocking collectives: 55.8 us -> 0 us
  starting transfers between devices: 40 us -> 0 us
  matrix products: 24.3 us -> 0 us
    gather x56 -> x0, local copies, waits for them, and re-layouts: 1690 us -> none  [neighbour_sum(): picked = jnp.take(padded, base + offsets[slot_index], axis=1)]
    convert_element_type x16 -> x0, other arithmetic: 242 us -> none  [the longest x6 192 us: chebyshev(): state = absorb(state, term_index, following.astype(jnp.bfloat16))]
    pallas_call x0 -> x2, Pallas kernels: none -> 89.7 us  [the longest x1 64.7 us: body(): pl.pallas_call(functools.partial(cheb_kernel, np_), out_shape=jax.ShapeDt...]
    concatenate x7 -> x0, local copies, waits for them, and re-layouts: 84.7 us -> none  [padded_2(): x = jnp.concatenate([before, x, after], axis=dim)]
    all_to_all x1 -> x0, blocking collectives: 49.7 us -> none  [body(): lax.all_to_all(outgoing, 'patch', split_axis=0, concat_axis=0, tiled=True)]
    ppermute x14 -> x0, starting transfers between devices: 40 us -> none  [the longest x7 25.3 us: padded_2(): before = lax.ppermute(last, axis, up)]
    dot_general x16 -> x0, matrix products: 24.3 us -> none  [absorb_groups(): jnp.dot(mine[term_index][:, group * width:(group + 1) * width], term_bf[g...]
  transfers between devices with their start and end apart: 15 -> 0, of which waited for: 1 -> 0; matrix products, arithmetic and copies ran while one was open for 2% -> 0% of each run, Pallas kernels for 0% -> 0%
where the time goes in v1:
time: 92.1 us; the launch traced here: 91.9 us
  Pallas kernels  89.7 us (97%)
  local copies, waits for them, and re-layouts  2.2 us (2%)
    pallas_call x1, Pallas kernels, body(): pl.pallas_call(functools.partial(cheb_kernel, np_), out_shape=jax.ShapeDt...  64.7 us
    pallas_call x1, Pallas kernels, body(): pl.pallas_call(functools.partial(dispatch_kernel, np_), out_shape=jax.Sha...  25 us
    unnamed x1, local copies, waits for them, and re-layouts  2.2 us

profile of v1, /device:TPU:1, one launch (start us, length us, event | category | flops | bytes accessed | tf_op | source)
XLA Modules:
  0.0 91.9 jit_solution(5705810046818619210)
XLA Ops:
  0.0 64.7 %cheb.1.out_ref = bf16[64,32,128]{2,1,0:T(8,128)(2,1)} custom-call(bf16[32,8192]{1,0:T(8,128)(2,1)} %feat.1, s32[8,8192]{1,0:T(8,128)} %offs.1, f32[8,8192]{1,0:T(8,128)} %wts.1, bf16[8,32,64]{2,1,0:T(8,128)(2,1)} %bitcast.9, f32[1,32]{1,0:T(1,128)} %bitcast.10, s32[1,32]{1,0:T(1,128)} %bitcast.11), custom_call_target="tpu_custom_call" | custom-call | tf_op jit(solution)/shard_map/cheb/pallas_call | solution.py:503
  64.7 25.0 %dispatch.1 = bf16[64,32,128]{2,1,0:T(8,128)(2,1)} custom-call(bf16[64,32,128]{2,1,0:T(8,128)(2,1)} %cheb.1.out_ref), custom_call_target="tpu_custom_call" | custom-call | tf_op jit(solution)/shard_map/dispatch/pallas_call | solution.py:522
  89.7 2.2 %copy.9 = bf16[1,64,2,2048]{3,2,1,0:T(2,128)(2,1)} copy(bf16[1,64,2,2048]{3,2,1,0:T(2,128)(2,1)} %bitcast.8) | data formatting | bytes 1048576

commit v2 on v1

--- a/solution.py
+++ b/solution.py
@@ -34,9 +34,12 @@
 
 
 def cheb_kernel(np_, feat, offs, wts, mix, bias, own_ref, out_ref,
-                tb, fp, wm, ot, wt, cor, s16, w16, x3, mixall, biasall, inv, inv_s,
-                msg, snd, t0_s, t0_r, tab_l, tab_s, tab_r, par_s, par_r,
-                in_s, in_r, mid_s, mid_r, sw_s, sw_r, loc):
+                tb0, tb1, tb2, tb3, tb4, tb5, tb6, fp0, fp1,
+                wm, ot, wt, cor, s16, w16, x3, mixall, biasall, inv, inv_s,
+                msg, snd, outg, t0_s, t0_r, tab_l, tab_s, tab_r, par_s, par_r,
+                in_s, in_r, mid_s, mid_r, sw_s, sw_r, loc, all_s, all_r):
+    tb = (tb0, tb1, tb2, tb3, tb4, tb5, tb6)
+    fp = (fp0, fp1)
     p = lax.axis_index("patch")
     g = lax.axis_index("chan")
     n, c = p // 2, p % 2
@@ -51,12 +54,12 @@
 
     outer = pl.multiple_of((1 - c) * 0 + c * (LANES - OUT_W), 128)
     for k in range(1, K - 1):
-        tb[k, :, pl.ds(outer, OUT_W)] = jnp.zeros((CH, OUT_W), BF)
+        tb[k][:, pl.ds(outer, OUT_W)] = jnp.zeros((CH, OUT_W), BF)
     at_end = (line == 0) | (line == last)
 
     @pl.when(at_end)
     def _():
-        tb[0, :, pl.ds(outer, OUT_W)] = jnp.zeros((CH, OUT_W), BF)
+        tb0[:, pl.ds(outer, OUT_W)] = jnp.zeros((CH, OUT_W), BF)
         to = pl.multiple_of(c * OWN * 256, 128)
         ot[:, pl.ds(to, EXT * 256)] = jnp.zeros((8, EXT * 256), jnp.int32)
         wt[:, pl.ds(to, EXT * 256)] = jnp.zeros((8, EXT * 256), F32)
@@ -72,7 +75,18 @@
                 @pl.when((n + dn >= 0) & (n + dn < ng) & ~((pp == p) & (dg == g)))
                 def _():
                     pl.semaphore_signal(bar, inc=1, device_id=(pp, dg), device_id_type=MESH)
-    pl.semaphore_wait(bar, 11 - 4 * jnp.where((n == 0) | (n == ng - 1), 1, 0))
+
+    def hello(i, carry):
+        j = (i + p) % np_
+        pp, gg = 2 * (j // 2) + g, j % 2
+
+        @pl.when(~((pp == p) & (gg == g)))
+        def _():
+            pl.semaphore_signal(bar, inc=1, device_id=(pp, gg), device_id_type=MESH)
+        return carry
+
+    lax.fori_loop(0, np_, hello, 0)
+    pl.semaphore_wait(bar, 11 - 4 * jnp.where((n == 0) | (n == ng - 1), 1, 0) + np_ - jnp.where(c == g, 1, 0))
 
     half = 4096
     main_dst = pl.multiple_of((1 - c) * EXT * 256, 128)
@@ -99,7 +113,7 @@
             dst.at[:, pl.ds(ext_dst, EXT * 256)], tab_l.at[i])
 
     out_line = line - 1 + 2 * c
-    outp, outg = place(out_line)
+    outp, outg_ = place(out_line)
     has_out = ~at_end
     other_ext = pl.multiple_of((1 - c) * OWN * 256, 128)
 
@@ -108,7 +122,7 @@
             src_ref=src.at[:, pl.ds(pl.multiple_of(c * (8192 - EXT * 256), 128), EXT * 256)],
             dst_ref=dst.at[:, pl.ds(other_ext, EXT * 256)],
             send_sem=tab_s.at[2 + i], recv_sem=tab_r.at[2 + i],
-            device_id=(outp, outg), device_id_type=MESH)
+            device_id=(outp, outg_), device_id_type=MESH)
 
     @pl.when(home)
     def _():
@@ -130,7 +144,7 @@
     def flow_parts(i):
         target, src0, size, dst0, sem = flows[i]
         src = feat.at[:, pl.ds(src0, size)]
-        dst = tb.at[0, pl.ds(row, 32), pl.ds(dst0, size)]
+        dst = tb0.at[pl.ds(row, 32), pl.ds(dst0, size)]
         return target, src, dst, sem + g
 
     def flow_ok(i):
@@ -249,46 +263,44 @@
     main_at = pl.multiple_of((1 - c) * (LANES - HALO - 4096), 128)
     for gg in range(2):
         pltpu.make_async_copy(feat.at[:, pl.ds(0, HALO + 4096)],
-                              tb.at[0, pl.ds(32 * gg, 32), pl.ds(main_at, HALO + 4096)],
+                              tb0.at[pl.ds(32 * gg, 32), pl.ds(main_at, HALO + 4096)],
                               t0_r.at[gg]).wait()
 
-        @pl.when(has_out)
-        def _():
-            pltpu.make_async_copy(feat.at[:, pl.ds(0, OUT_W)],
-                                  tb.at[0, pl.ds(32 * gg, 32), pl.ds(outer, OUT_W)],
-                                  t0_r.at[2 + gg]).wait()
-
-    def block(k, i):
+    def term(k, i):
         b = block_of(i)
         at = pl.multiple_of(256 * b, 256)
-        win = tb[k - 1, :, pl.ds(at + 128, WIN)]
-        u = jnp.dot(win, wm[b], preferred_element_type=F32)
-        left = pltpu.roll(tb[k - 1, :, pl.ds(at, 128)].astype(F32), 1, 1)
-        right = pltpu.roll(tb[k - 1, :, pl.ds(at + 1408, 128)].astype(F32), 127, 1)
+        src = tb[k - 1]
+        u = jnp.dot(src[:, pl.ds(at + 128, WIN)], wm[b], preferred_element_type=F32)
+        left = pltpu.roll(src[:, pl.ds(at, 128)].astype(F32), 1, 1)
+        right = pltpu.roll(src[:, pl.ds(at + 1408, 128)].astype(F32), 127, 1)
         u = u + jnp.concatenate([left * cor[b, 0:1, 0:128], right * cor[b, 1:2, 128:256]], axis=1)
         if k == 1:
             t = u
         elif k == 2:
-            t = 2.0 * u - tb[0, :, pl.ds(at + HALO, 256)].astype(F32)
+            t = 2.0 * u - tb0[:, pl.ds(at + HALO, 256)].astype(F32)
         else:
-            t = 2.0 * u - fp[k % 2, :, pl.ds(at, 256)]
-        if k < K - 1:
-            fp[k % 2, :, pl.ds(at, 256)] = t
-        tb[k, :, pl.ds(at + HALO, 256)] = t.astype(BF)
-
-    def run(k, lo, hi, group=4):
+            t = 2.0 * u - fp[k % 2][:, pl.ds(at, 256)]
+        return at, t
+
+    def run(k, lo, hi, group=10):
+        def one(i):
+            at, t = term(k, i)
+            fp[k % 2][:, pl.ds(at, 256)] = t
+            tb[k][:, pl.ds(at + HALO, 256)] = t.astype(BF)
+
         full = (hi - lo) // group
 
         def some(m, carry):
             for r in range(group):
-                block(k, lo + m * group + r)
+                one(lo + m * group + r)
             return carry
 
+        first = lo
         if full > 1:
             lax.fori_loop(0, full, some, 0)
-            lo = lo + full * group
-        for i in range(lo, hi):
-            block(k, i)
+            first = lo + full * group
+        for i in range(first, hi):
+            one(i)
 
     own_at = HALO + (1 - c) * EXT * 256
     edge_src = pl.multiple_of(own_at + (1 - c) * (4096 - HALO), 128)
@@ -296,7 +308,7 @@
 
     def inner(k):
         return pltpu.make_async_remote_copy(
-            src_ref=tb.at[k, :, pl.ds(edge_src, HALO)], dst_ref=tb.at[k, :, pl.ds(edge_dst, HALO)],
+            src_ref=tb[k].at[:, pl.ds(edge_src, HALO)], dst_ref=tb[k].at[:, pl.ds(edge_dst, HALO)],
             send_sem=in_s.at[k], recv_sem=in_r.at[k], device_id=sib, device_id_type=MESH)
 
     def outer_copy(k, width, m):
@@ -304,14 +316,23 @@
         if k == 3:
             dst = x3.at[:, :]
         else:
-            dst = tb.at[k, :, pl.ds(pl.multiple_of((1 - c) * (LANES - OUT_W) + c * (OUT_W - width), 128), width)]
+            dst = tb[k].at[:, pl.ds(pl.multiple_of((1 - c) * (LANES - OUT_W) + c * (OUT_W - width), 128), width)]
         return pltpu.make_async_remote_copy(
-            src_ref=tb.at[k, :, pl.ds(src, width)], dst_ref=dst,
-            send_sem=mid_s.at[m], recv_sem=mid_r.at[m], device_id=(outp, outg), device_id_type=MESH)
+            src_ref=tb[k].at[:, pl.ds(src, width)], dst_ref=dst,
+            send_sem=mid_s.at[m], recv_sem=mid_r.at[m], device_id=(outp, outg_), device_id_type=MESH)
 
     run(1, 0, 3)
     inner(1).start()
-    run(1, 3, 23)
+    run(1, 3, 13)
+
+    @pl.when(has_out)
+    def _():
+        for gg in range(2):
+            pltpu.make_async_copy(feat.at[:, pl.ds(0, OUT_W)],
+                                  tb0.at[pl.ds(32 * gg, 32), pl.ds(outer, OUT_W)],
+                                  t0_r.at[2 + gg]).wait()
+
+    run(1, 13, 23)
     inner(1).wait_recv()
     run(2, 0, 3)
     inner(2).start()
@@ -325,37 +346,11 @@
     def _():
         outer_copy(3, S3, 0).start()
 
-    inner(3).wait_recv()
     run(4, 9, 16)
 
     @pl.when(has_out)
     def _():
         outer_copy(4, S4, 1).start()
-
-    run(4, 0, 3)
-    inner(4).start()
-    run(4, 3, 9)
-    inner(4).wait_recv()
-    run(5, 0, 3)
-    inner(5).start()
-    run(5, 3, 13)
-
-    @pl.when(has_out)
-    def _():
-        outer_copy(3, S3, 0).wait_recv()
-        outer_copy(4, S4, 1).wait_recv()
-        d3 = pl.multiple_of((1 - c) * (EXT * 256 - S3) + c * OWN * 256, 128)
-        fp[1, :, pl.ds(d3, S3)] = x3[...].astype(F32)
-        d4 = pl.multiple_of((1 - c) * (EXT * 256 - 768) + c * OWN * 256, 128)
-        fp[0, :, pl.ds(d4, 768)] = tb[4, :, pl.ds(d4 + HALO, 768)].astype(F32)
-
-    run(5, 13, 21)
-    inner(5).wait_recv()
-    run(6, 0, 3)
-    inner(6).start()
-    run(6, 3, 19)
-    inner(6).wait_recv()
-    run(7, 0, 16)
 
     pltpu.make_async_copy(mixall.at[1 - g], mixall.at[1 - g], par_r.at[0]).wait()
     pltpu.make_async_copy(biasall.at[1 - g], biasall.at[1 - g], par_r.at[1]).wait()
@@ -367,49 +362,93 @@
     bcol = jnp.sum(jnp.where(l1 == 2 * (o1 % 16) + o1 // 32, brow, 0.0), axis=1, keepdims=True)
     pi, pq = iota((512, 128), 0), iota((512, 128), 1)
     pool = jnp.where(pi % 256 // 4 + 64 * (pi // 256) == pq, 0.25, 0.0).astype(BF)
-
-    def finish(b, carry):
-        at = pl.multiple_of(own_at + 256 * b, 128)
+    to_smem.wait()
+
+    inner(3).wait_recv()
+    run(4, 0, 3)
+    inner(4).start()
+    run(4, 3, 9)
+    inner(4).wait_recv()
+    run(5, 0, 3)
+    inner(5).start()
+    run(5, 3, 13)
+    inner(5).wait_recv()
+    run(6, 0, 3)
+    inner(6).start()
+    run(6, 3, 10)
+    inner(6).wait_recv()
+
+    def finish(i):
+        at, t = term(7, i)
+        t = t.astype(BF)
         total = bcol
         for gg in range(2):
-            rhs = jnp.concatenate([tb[k, 32 * gg:32 * gg + 32, pl.ds(at, 256)] for k in range(K)], axis=0)
+            rows = slice(32 * gg, 32 * gg + 32)
+            rhs = jnp.concatenate([tb[k][rows, pl.ds(at + HALO, 256)] for k in range(K - 1)] + [t[rows]], axis=0)
             part = jnp.dot(mixall[gg], rhs, preferred_element_type=F32)
             total = total + part.astype(BF).astype(F32)
         filt = jnp.maximum(total, 0.0).astype(BF)
         lhs = jnp.concatenate([filt[0:32], filt[32:64]], axis=1)
-        pooled = jnp.dot(lhs, pool, preferred_element_type=F32).astype(BF)
-        sel = jnp.where(c == 0, pooled[0:16].astype(F32), pooled[16:32].astype(F32)).astype(BF)
-        oth = jnp.where(c == 0, pooled[16:32].astype(F32), pooled[0:16].astype(F32)).astype(BF)
-        msg[c * OWN + b] = sel
-        snd[b] = oth
-        return carry
+        pooled = jnp.dot(lhs, pool, preferred_element_type=F32)
+        b = block_of(i) - (1 - c) * EXT
+        msg[c * OWN + b] = jnp.where(c == 0, pooled[0:16], pooled[16:32]).astype(BF)
+        snd[b] = jnp.where(c == 0, pooled[16:32], pooled[0:16]).astype(BF)
 
     def swap(m):
-        part = pl.ds(pl.multiple_of(8 * m, 8), 8)
+        b0 = c * 8 * m + (1 - c) * (8 - 8 * m)
         return pltpu.make_async_remote_copy(
-            src_ref=snd.at[part], dst_ref=msg.at[pl.ds(c * OWN + 8 * m, 8)],
+            src_ref=snd.at[pl.ds(b0, 8)], dst_ref=msg.at[pl.ds(c * OWN + b0, 8)],
             send_sem=sw_s.at[m], recv_sem=sw_r.at[m], device_id=sib, device_id_type=MESH)
 
-    for m in range(2):
-        for r in range(8):
-            finish(8 * m + r, 0)
-        swap(m).start()
-    to_smem.wait()
+    for i in range(0, 7):
+        finish(i)
+
+    @pl.when(has_out)
+    def _():
+        outer_copy(3, S3, 0).wait_recv()
+        outer_copy(4, S4, 1).wait_recv()
+        d3 = pl.multiple_of((1 - c) * (EXT * 256 - S3) + c * OWN * 256, 128)
+        fp1[:, pl.ds(d3, S3)] = x3[...].astype(F32)
+        d4 = pl.multiple_of((1 - c) * (EXT * 256 - 768) + c * OWN * 256, 128)
+        fp0[:, pl.ds(d4, 768)] = tb4[:, pl.ds(d4 + HALO, 768)].astype(F32)
+
+    run(5, 13, 21)
+    run(6, 10, 19)
+    finish(7)
+    swap(0).start()
+    for i in range(8, 16):
+        finish(i)
+    swap(1).start()
     for m in range(2):
         pltpu.make_async_copy(msg.at[pl.ds((1 - c) * OWN + 8 * m, 8)],
                               msg.at[pl.ds((1 - c) * OWN + 8 * m, 8)], sw_r.at[m]).wait()
 
     ei, ej = iota((32, 32), 0), iota((32, 32), 1)
     weave = jnp.where(ej == (ei % 2) * 16 + ei // 2, 1.0, 0.0).astype(BF)
-
-    def assemble(m, carry):
+    src_patch = 2 * n + gx
+
+    def assemble(i, carry):
+        m = (i + p // 4) % (np_ // 4)
         cols = []
         for r in range(4):
             o = 4 * m + r
             cols.append(jnp.concatenate([msg[inv_s[0, 2 * o]], msg[inv_s[0, 2 * o + 1]]], axis=0))
         res = jnp.dot(weave, jnp.concatenate(cols, axis=1), preferred_element_type=F32).astype(BF)
         for r in range(4):
-            out_ref[4 * m + r] = res[:, 128 * r:128 * (r + 1)]
+            outg[4 * m + r] = res[:, 128 * r:128 * (r + 1)]
+        for r in range(4):
+            o = 4 * m + r
+            me = (o == p) & (c == g)
+
+            @pl.when(me)
+            def _():
+                pltpu.make_async_copy(outg.at[o], out_ref.at[src_patch], all_r.at[0]).start()
+
+            @pl.when(~me)
+            def _():
+                pltpu.make_async_remote_copy(
+                    src_ref=outg.at[o], dst_ref=out_ref.at[src_patch], send_sem=all_s.at[0],
+                    recv_sem=all_r.at[0], device_id=(o, c), device_id_type=MESH).start()
         return carry
 
     lax.fori_loop(0, np_ // 4, assemble, 0)
@@ -440,95 +479,38 @@
     for m in range(2):
         swap(m).wait_send()
 
-
-def dispatch_kernel(np_, out_ref, got_ref, ss, rs):
-    p = lax.axis_index("patch")
-    g = lax.axis_index("chan")
-    n, c = p // 2, p % 2
-    src = 2 * n + (g + n) % 2
-    bar = pltpu.get_barrier_semaphore()
-
-    def hello(i, carry):
-        j = (i + p) % np_
-        pp = 2 * (j // 2) + g
-        gg = j % 2
-
-        @pl.when(~((pp == p) & (gg == g)))
-        def _():
-            pl.semaphore_signal(bar, inc=1, device_id=(pp, gg), device_id_type=MESH)
-        return carry
-
-    lax.fori_loop(0, np_, hello, 0)
-    pl.semaphore_wait(bar, np_ - jnp.where(c == g, 1, 0))
-
-    def copy(o):
-        return pltpu.make_async_remote_copy(
-            src_ref=out_ref.at[o], dst_ref=got_ref.at[src], send_sem=ss.at[o], recv_sem=rs.at[src],
-            device_id=(o, c), device_id_type=MESH)
-
-    def send(i, carry):
-        o = (p + i) % np_
-        me = (o == p) & (c == g)
-
-        @pl.when(me)
-        def _():
-            pltpu.make_async_copy(out_ref.at[o], got_ref.at[src], rs.at[src]).start()
-
-        @pl.when(~me)
-        def _():
-            copy(o).start()
-        return carry
-
-    lax.fori_loop(0, np_, send, 0)
-
-    def take(i, carry):
-        pltpu.make_async_copy(got_ref.at[i], got_ref.at[i], rs.at[i]).wait()
-        return carry
-
-    lax.fori_loop(0, np_, take, 0)
-
-    def sent(o, carry):
-        @pl.when(~((o == p) & (c == g)))
-        def _():
-            copy(o).wait_send()
-        return carry
-
-    lax.fori_loop(0, np_, sent, 0)
+    pltpu.make_async_copy(out_ref.at[:], out_ref.at[:], all_r.at[0]).wait()
+    pltpu.make_async_copy(outg.at[pl.ds(0, np_ - 1)], outg.at[pl.ds(0, np_ - 1)], all_s.at[0]).wait()
+
+    @pl.when(c != g)
+    def _():
+        pltpu.make_async_copy(outg.at[0], outg.at[0], all_s.at[0]).wait()
 
 
 def body(features, offsets, edge_weights, mix, bias, owners):
     np_ = lax.axis_size("patch")
     any_, vmem = pl.BlockSpec(memory_space=pl.ANY), pl.BlockSpec(memory_space=pltpu.VMEM)
     dma, vm = pltpu.SemaphoreType.DMA, pltpu.VMEM
-    out = pl.pallas_call(
+    got = pl.pallas_call(
         functools.partial(cheb_kernel, np_),
         out_shape=jax.ShapeDtypeStruct((np_, 32, 128), BF),
         in_specs=[any_, any_, any_, vmem, vmem, vmem],
         out_specs=vmem,
         scratch_shapes=[
-            vm((K, CH, LANES), BF), vm((2, CH, NPX), F32), vm((NB, WIN, 256), BF),
+            *[vm((CH, LANES), BF)] * (K - 1), *[vm((CH, NPX), F32)] * 2, vm((NB, WIN, 256), BF),
             vm((8, NPX), jnp.int32), vm((8, NPX), F32), vm((NB, 8, 256), F32),
             vm((8, 16, 256), jnp.int16), vm((8, 16, 256), BF), vm((CH, S3), BF),
             vm((2, 64, 256), BF), vm((2, 8, 128), F32), vm((2, 8, 128), jnp.int32),
             pltpu.SMEM((8, 128), jnp.int32),
-            vm((2 * OWN + 1, 16, 128), BF), vm((OWN, 16, 128), BF),
+            vm((2 * OWN + 1, 16, 128), BF), vm((OWN, 16, 128), BF), vm((np_, 32, 128), BF),
             dma((4,)), dma((4,)), dma((2,)), dma((4,)), dma((4,)), dma((3,)), dma((3,)),
             dma((K,)), dma((K,)), dma((2,)), dma((2,)), dma((2,)), dma((2,)), dma((1,)),
+            dma((1,)), dma((1,)),
         ],
         compiler_params=pltpu.CompilerParams(
             vmem_limit_bytes=62 << 20, collective_id=0, has_side_effects=True),
         name="cheb",
     )(features, offsets, edge_weights, mix.transpose(0, 2, 1), bias.reshape(1, -1), owners.reshape(1, -1))
-    got = pl.pallas_call(
-        functools.partial(dispatch_kernel, np_),
-        out_shape=jax.ShapeDtypeStruct((np_, 32, 128), BF),
-        in_specs=[any_],
-        out_specs=any_,
-        scratch_shapes=[dma((np_,)), dma((np_,))],
-        compiler_params=pltpu.CompilerParams(
-            vmem_limit_bytes=62 << 20, collective_id=1, has_side_effects=True),
-        name="dispatch",
-    )(out)
     got = got.reshape(np_, 16, 2, 128).transpose(0, 2, 1, 3).reshape(np_, 2, 2048)
     return got[None]
 

time: 92.1 us -> 64.2 us (0.70)
  Pallas kernels: 89.7 us -> 61.5 us
    pallas_call x1 -> x0, Pallas kernels: 25 us -> none  [body(): pl.pallas_call(functools.partial(dispatch_kernel, np_), out_shape=jax.Sha...]
    pallas_call x1, Pallas kernels: 64.7 us -> 61.5 us  [body(): pl.pallas_call(functools.partial(cheb_kernel, np_), out_shape=jax.ShapeDt...]
where the time goes in v2:
time: 64.2 us; the launch traced here: 63.7 us
  Pallas kernels  61.5 us (96%)
  local copies, waits for them, and re-layouts  2.2 us (3%)
    pallas_call x1, Pallas kernels, body(): pl.pallas_call(functools.partial(cheb_kernel, np_), out_shape=jax.ShapeDt...  61.5 us
    unnamed x1, local copies, waits for them, and re-layouts  2.2 us

profile of v2, /device:TPU:1, one launch (start us, length us, event | category | flops | bytes accessed | tf_op | source)
XLA Modules:
  0.0 63.7 jit_solution(11561705193348808670)
XLA Ops:
  0.0 61.5 %cheb.1 = bf16[64,32,128]{2,1,0:T(8,128)(2,1)} custom-call(bf16[32,8192]{1,0:T(8,128)(2,1)} %feat.1, s32[8,8192]{1,0:T(8,128)} %offs.1, f32[8,8192]{1,0:T(8,128)} %wts.1, bf16[8,32,64]{2,1,0:T(8,128)(2,1)} %bitcast.9, f32[1,32]{1,0:T(1,128)} %bitcast.10, s32[1,32]{1,0:T(1,128)} %bitcast.11), custom_call_target="tpu_custom_call" | custom-call | tf_op jit(solution)/shard_map/cheb/pallas_call | solution.py:494
  61.5 2.2 %copy.9 = bf16[1,64,2,2048]{3,2,1,0:T(2,128)(2,1)} copy(bf16[1,64,2,2048]{3,2,1,0:T(2,128)(2,1)} %bitcast.8) | data formatting | bytes 1048576

commit v3 on v2

--- a/solution.py
+++ b/solution.py
@@ -13,15 +13,14 @@
 K = 8
 CH = 64
 OWN = 16
-EXT = 7
+EXT = 5
 NB = OWN + EXT
 HALO = 640
 LANES = HALO + NB * 256 + HALO
 OUT_W = EXT * 256 + HALO
 WIN = 1280
 NPX = NB * 256
-S3 = 1152
-S4 = 1664
+MID = 1152
 
 
 def place(line):
@@ -35,8 +34,8 @@
 
 def cheb_kernel(np_, feat, offs, wts, mix, bias, own_ref, out_ref,
                 tb0, tb1, tb2, tb3, tb4, tb5, tb6, fp0, fp1,
-                wm, ot, wt, cor, s16, w16, x3, mixall, biasall, inv, inv_s,
-                msg, snd, outg, t0_s, t0_r, tab_l, tab_s, tab_r, par_s, par_r,
+                wm, ot, wt, cor, s16, w16, mixall, biasall, inv, inv_s,
+                msg, snd, outg, plhs, t0_s, t0_r, tab_l, tab_s, tab_r, par_s, par_r,
                 in_s, in_r, mid_s, mid_r, sw_s, sw_r, loc, all_s, all_r):
     tb = (tb0, tb1, tb2, tb3, tb4, tb5, tb6)
     fp = (fp0, fp1)
@@ -270,10 +269,12 @@
         b = block_of(i)
         at = pl.multiple_of(256 * b, 256)
         src = tb[k - 1]
-        u = jnp.dot(src[:, pl.ds(at + 128, WIN)], wm[b], preferred_element_type=F32)
+        win = src[:, pl.ds(at + 128, WIN)]
         left = pltpu.roll(src[:, pl.ds(at, 128)].astype(F32), 1, 1)
         right = pltpu.roll(src[:, pl.ds(at + 1408, 128)].astype(F32), 127, 1)
-        u = u + jnp.concatenate([left * cor[b, 0:1, 0:128], right * cor[b, 1:2, 128:256]], axis=1)
+        u0 = jnp.dot(win, wm[b, :, 0:128], preferred_element_type=F32) + left * cor[b, 0:1, 0:128]
+        u1 = jnp.dot(win, wm[b, :, 128:256], preferred_element_type=F32) + right * cor[b, 1:2, 128:256]
+        u = jnp.concatenate([u0, u1], axis=1)
         if k == 1:
             t = u
         elif k == 2:
@@ -311,15 +312,12 @@
             src_ref=tb[k].at[:, pl.ds(edge_src, HALO)], dst_ref=tb[k].at[:, pl.ds(edge_dst, HALO)],
             send_sem=in_s.at[k], recv_sem=in_r.at[k], device_id=sib, device_id_type=MESH)
 
-    def outer_copy(k, width, m):
-        src = pl.multiple_of(own_at + c * (4096 - width), 128)
-        if k == 3:
-            dst = x3.at[:, :]
-        else:
-            dst = tb[k].at[:, pl.ds(pl.multiple_of((1 - c) * (LANES - OUT_W) + c * (OUT_W - width), 128), width)]
+    def mid(k):
+        src = pl.multiple_of(own_at + c * (4096 - MID), 128)
+        dst = pl.multiple_of((1 - c) * (LANES - OUT_W) + c * (OUT_W - MID), 128)
         return pltpu.make_async_remote_copy(
-            src_ref=tb[k].at[:, pl.ds(src, width)], dst_ref=dst,
-            send_sem=mid_s.at[m], recv_sem=mid_r.at[m], device_id=(outp, outg_), device_id_type=MESH)
+            src_ref=tb[k].at[:, pl.ds(src, MID)], dst_ref=tb[k].at[:, pl.ds(dst, MID)],
+            send_sem=mid_s.at[k // 4], recv_sem=mid_r.at[k // 4], device_id=(outp, outg_), device_id_type=MESH)
 
     run(1, 0, 3)
     inner(1).start()
@@ -332,25 +330,17 @@
                                   tb0.at[pl.ds(32 * gg, 32), pl.ds(outer, OUT_W)],
                                   t0_r.at[2 + gg]).wait()
 
-    run(1, 13, 23)
+    run(1, 13, NB)
     inner(1).wait_recv()
     run(2, 0, 3)
     inner(2).start()
-    run(2, 3, 21)
+    run(2, 3, 19)
     inner(2).wait_recv()
-    run(3, 0, 3)
-    inner(3).start()
-    run(3, 3, 19)
+    run(3, 11, 16)
 
     @pl.when(has_out)
     def _():
-        outer_copy(3, S3, 0).start()
-
-    run(4, 9, 16)
-
-    @pl.when(has_out)
-    def _():
-        outer_copy(4, S4, 1).start()
+        mid(3).start()
 
     pltpu.make_async_copy(mixall.at[1 - g], mixall.at[1 - g], par_r.at[0]).wait()
     pltpu.make_async_copy(biasall.at[1 - g], biasall.at[1 - g], par_r.at[1]).wait()
@@ -364,18 +354,33 @@
     pool = jnp.where(pi % 256 // 4 + 64 * (pi // 256) == pq, 0.25, 0.0).astype(BF)
     to_smem.wait()
 
+    run(3, 0, 3)
+    inner(3).start()
+    run(3, 3, 11)
     inner(3).wait_recv()
     run(4, 0, 3)
     inner(4).start()
-    run(4, 3, 9)
+    run(4, 3, 13)
     inner(4).wait_recv()
     run(5, 0, 3)
     inner(5).start()
-    run(5, 3, 13)
+    run(5, 3, 10)
     inner(5).wait_recv()
     run(6, 0, 3)
     inner(6).start()
-    run(6, 3, 10)
+
+    @pl.when(has_out)
+    def _():
+        mid(3).wait_recv()
+
+    run(4, 13, 19)
+    run(5, 10, 16)
+
+    @pl.when(has_out)
+    def _():
+        mid(5).start()
+
+    run(6, 3, 13)
     inner(6).wait_recv()
 
     def finish(i):
@@ -388,11 +393,16 @@
             part = jnp.dot(mixall[gg], rhs, preferred_element_type=F32)
             total = total + part.astype(BF).astype(F32)
         filt = jnp.maximum(total, 0.0).astype(BF)
-        lhs = jnp.concatenate([filt[0:32], filt[32:64]], axis=1)
-        pooled = jnp.dot(lhs, pool, preferred_element_type=F32)
-        b = block_of(i) - (1 - c) * EXT
-        msg[c * OWN + b] = jnp.where(c == 0, pooled[0:16], pooled[16:32]).astype(BF)
-        snd[b] = jnp.where(c == 0, pooled[16:32], pooled[0:16]).astype(BF)
+        plhs[32 * i:32 * i + 32, 0:256] = filt[0:32]
+        plhs[32 * i:32 * i + 32, 256:512] = filt[32:64]
+
+    def pool_blocks(m):
+        pooled = jnp.dot(plhs[256 * m:256 * m + 256, :], pool, preferred_element_type=F32)
+        for r in range(8):
+            b = block_of(8 * m + r) - (1 - c) * EXT
+            even, odd = pooled[32 * r:32 * r + 16], pooled[32 * r + 16:32 * r + 32]
+            msg[c * OWN + b] = jnp.where(c == 0, even, odd).astype(BF)
+            snd[b] = jnp.where(c == 0, odd, even).astype(BF)
 
     def swap(m):
         b0 = c * 8 * m + (1 - c) * (8 - 8 * m)
@@ -400,24 +410,21 @@
             src_ref=snd.at[pl.ds(b0, 8)], dst_ref=msg.at[pl.ds(c * OWN + b0, 8)],
             send_sem=sw_s.at[m], recv_sem=sw_r.at[m], device_id=sib, device_id_type=MESH)
 
-    for i in range(0, 7):
+    for i in range(0, 8):
         finish(i)
+    pool_blocks(0)
+    swap(0).start()
+    for i in range(8, 10):
+        finish(i)
 
     @pl.when(has_out)
     def _():
-        outer_copy(3, S3, 0).wait_recv()
-        outer_copy(4, S4, 1).wait_recv()
-        d3 = pl.multiple_of((1 - c) * (EXT * 256 - S3) + c * OWN * 256, 128)
-        fp1[:, pl.ds(d3, S3)] = x3[...].astype(F32)
-        d4 = pl.multiple_of((1 - c) * (EXT * 256 - 768) + c * OWN * 256, 128)
-        fp0[:, pl.ds(d4, 768)] = tb4[:, pl.ds(d4 + HALO, 768)].astype(F32)
-
-    run(5, 13, 21)
-    run(6, 10, 19)
-    finish(7)
-    swap(0).start()
-    for i in range(8, 16):
+        mid(5).wait_recv()
+
+    run(6, 13, 19)
+    for i in range(10, 16):
         finish(i)
+    pool_blocks(1)
     swap(1).start()
     for m in range(2):
         pltpu.make_async_copy(msg.at[pl.ds((1 - c) * OWN + 8 * m, 8)],
@@ -473,8 +480,8 @@
 
     @pl.when(has_out)
     def _():
-        outer_copy(3, S3, 0).wait_send()
-        outer_copy(4, S4, 1).wait_send()
+        mid(3).wait_send()
+        mid(5).wait_send()
 
     for m in range(2):
         swap(m).wait_send()
@@ -499,10 +506,10 @@
         scratch_shapes=[
             *[vm((CH, LANES), BF)] * (K - 1), *[vm((CH, NPX), F32)] * 2, vm((NB, WIN, 256), BF),
             vm((8, NPX), jnp.int32), vm((8, NPX), F32), vm((NB, 8, 256), F32),
-            vm((8, 16, 256), jnp.int16), vm((8, 16, 256), BF), vm((CH, S3), BF),
+            vm((8, 16, 256), jnp.int16), vm((8, 16, 256), BF),
             vm((2, 64, 256), BF), vm((2, 8, 128), F32), vm((2, 8, 128), jnp.int32),
             pltpu.SMEM((8, 128), jnp.int32),
-            vm((2 * OWN + 1, 16, 128), BF), vm((OWN, 16, 128), BF), vm((np_, 32, 128), BF),
+            vm((2 * OWN + 1, 16, 128), BF), vm((OWN, 16, 128), BF), vm((np_, 32, 128), BF), vm((OWN * 32, 512), BF),
             dma((4,)), dma((4,)), dma((2,)), dma((4,)), dma((4,)), dma((3,)), dma((3,)),
             dma((K,)), dma((K,)), dma((2,)), dma((2,)), dma((2,)), dma((2,)), dma((1,)),
             dma((1,)), dma((1,)),

time: 64.2 us -> 58 us (0.903)
  Pallas kernels: 61.5 us -> 54.8 us
    pallas_call x1, Pallas kernels: 61.5 us -> 54.8 us  [body(): pl.pallas_call(functools.partial(cheb_kernel, np_), out_shape=jax.ShapeDt...]
where the time goes in v3:
time: 58 us; the launch traced here: 57 us
  Pallas kernels  54.8 us (94%)
  local copies, waits for them, and re-layouts  2.2 us (4%)
    pallas_call x1, Pallas kernels, body(): pl.pallas_call(functools.partial(cheb_kernel, np_), out_shape=jax.ShapeDt...  54.8 us
    unnamed x1, local copies, waits for them, and re-layouts  2.2 us

profile of v3, /device:TPU:1, one launch (start us, length us, event | category | flops | bytes accessed | tf_op | source)
XLA Modules:
  0.0 57.0 jit_solution(5904996725062294066)
XLA Ops:
  0.0 54.8 %cheb.1 = bf16[64,32,128]{2,1,0:T(8,128)(2,1)} custom-call(bf16[32,8192]{1,0:T(8,128)(2,1)} %feat.1, s32[8,8192]{1,0:T(8,128)} %offs.1, f32[8,8192]{1,0:T(8,128)} %wts.1, bf16[8,32,64]{2,1,0:T(8,128)(2,1)} %bitcast.9, f32[1,32]{1,0:T(1,128)} %bitcast.10, s32[1,32]{1,0:T(1,128)} %bitcast.11), custom_call_target="tpu_custom_call" | custom-call | tf_op jit(solution)/shard_map/cheb/pallas_call | solution.py:501
  54.8 2.2 %copy.9 = bf16[1,64,2,2048]{3,2,1,0:T(2,128)(2,1)} copy(bf16[1,64,2,2048]{3,2,1,0:T(2,128)(2,1)} %bitcast.8) | data formatting | bytes 1048576

commit v4 on v3

--- a/solution.py
+++ b/solution.py
@@ -52,7 +52,7 @@
     ng = np_ // 2
 
     outer = pl.multiple_of((1 - c) * 0 + c * (LANES - OUT_W), 128)
-    for k in range(1, K - 1):
+    for k in (3, 5):
         tb[k][:, pl.ds(outer, OUT_W)] = jnp.zeros((CH, OUT_W), BF)
     at_end = (line == 0) | (line == last)
 
@@ -157,20 +157,26 @@
             src_ref=src, dst_ref=dst, send_sem=t0_s.at[i], recv_sem=t0_r.at[sem],
             device_id=(tp, tg), device_id_type=MESH)
 
-    for i in range(4):
-        target, src, dst, sem = flow_parts(i)
-
-        @pl.when(flow_ok(i) & (target == line))
-        def _():
-            pltpu.make_async_copy(src, dst, t0_r.at[sem]).start()
-
-        @pl.when(flow_ok(i) & (target != line))
-        def _():
-            flow_remote(i).start()
+    def start_flows(which):
+        for i in which:
+            target, src, dst, sem = flow_parts(i)
+
+            @pl.when(flow_ok(i) & (target == line))
+            def _():
+                pltpu.make_async_copy(src, dst, t0_r.at[sem]).start()
+
+            @pl.when(flow_ok(i) & (target != line))
+            def _():
+                flow_remote(i).start()
+
+    start_flows((0, 1))
 
     @pl.when(home & has_out)
     def _():
         tables(lambda i, s, d: tab_ext_remote(i, s, d).start())
+
+    for k in (1, 2, 4, 6):
+        tb[k][:, pl.ds(outer, OUT_W)] = jnp.zeros((CH, OUT_W), BF)
 
     mixcat = jnp.concatenate([mix[k] for k in range(K)], axis=0)
     oi, oo = iota((64, 64), 0), iota((64, 64), 1)
@@ -205,7 +211,7 @@
     def block_of(i):
         return c * i + (1 - c) * (NB - 1 - i)
 
-    base = [(iota((16, 256), 0) + 16 * r).astype(jnp.int16) for r in range(16)]
+    base = [(iota((16, 128), 0) + 16 * r).astype(jnp.int16) for r in range(16)]
 
     def build(i, carry):
         b = block_of(i)
@@ -222,14 +228,19 @@
         for j in range(8):
             s16[j] = jnp.broadcast_to(s[j:j + 1], (16, 256)).astype(jnp.int16)
             w16[j] = jnp.broadcast_to(full[j:j + 1], (16, 256)).astype(BF)
-        for q in range(WIN // 256):
-            acc = [jnp.zeros((16, 256), BF)] * 16
-            for j in range(8):
-                sq = s16[j] - jnp.int16(256 * q)
-                wq = w16[j]
-                acc = [jnp.where(base[r] == sq, wq, acc[r]) for r in range(16)]
-            for r in range(16):
-                wm[b, 256 * q + 16 * r:256 * q + 16 * (r + 1), :] = acc[r]
+        for h in range(2):
+            px = slice(128 * h, 128 * h + 128)
+            first, stop = (0, 73) if h == 0 else (7, 80)
+            wm[b, slice(16 * stop, WIN) if h == 0 else slice(0, 16 * first), px] = jnp.zeros((112, 128), BF)
+            for q in range(first, stop, 16):
+                rows = range(min(16, stop - q))
+                acc = [jnp.zeros((16, 128), BF) for r in rows]
+                for j in range(8):
+                    sq = s16[j, :, px] - jnp.int16(16 * q)
+                    wq = w16[j, :, px]
+                    acc = [jnp.where(base[r] == sq, wq, acc[r]) for r in rows]
+                for r in rows:
+                    wm[b, 16 * (q + r):16 * (q + r + 1), px] = acc[r]
         return carry
 
     lo1 = jnp.where(home, 0, OWN)
@@ -245,7 +256,9 @@
     def _():
         tables(lambda i, s, d: tab_ext_local(i, s, d).wait())
 
-    lax.fori_loop(lo1, hi1, build, 0)
+    lax.fori_loop(lo1, lo1 + 5, build, 0)
+    start_flows((2, 3))
+    lax.fori_loop(lo1 + 5, hi1, build, 0)
 
     @pl.when(~home)
     def _():
@@ -494,6 +507,23 @@
         pltpu.make_async_copy(outg.at[0], outg.at[0], all_s.at[0]).wait()
 
 
+def copy_kernel(src, dst, buf, sa, sb):
+    step = src.shape[0] // 8
+
+    def part(ref, i):
+        return ref.at[pl.ds(i * step, step)]
+
+    ins = [pltpu.make_async_copy(part(src, i), part(buf, i), sa.at[i]) for i in range(8)]
+    outs = [pltpu.make_async_copy(part(buf, i), part(dst, i), sb.at[i]) for i in range(8)]
+    for cp in ins:
+        cp.start()
+    for i in range(8):
+        ins[i].wait()
+        outs[i].start()
+    for cp in outs:
+        cp.wait()
+
+
 def body(features, offsets, edge_weights, mix, bias, owners):
     np_ = lax.axis_size("patch")
     any_, vmem = pl.BlockSpec(memory_space=pl.ANY), pl.BlockSpec(memory_space=pltpu.VMEM)
@@ -502,7 +532,7 @@
         functools.partial(cheb_kernel, np_),
         out_shape=jax.ShapeDtypeStruct((np_, 32, 128), BF),
         in_specs=[any_, any_, any_, vmem, vmem, vmem],
-        out_specs=vmem,
+        out_specs=any_,
         scratch_shapes=[
             *[vm((CH, LANES), BF)] * (K - 1), *[vm((CH, NPX), F32)] * 2, vm((NB, WIN, 256), BF),
             vm((8, NPX), jnp.int32), vm((8, NPX), F32), vm((NB, 8, 256), F32),
@@ -518,6 +548,15 @@
             vmem_limit_bytes=62 << 20, collective_id=0, has_side_effects=True),
         name="cheb",
     )(features, offsets, edge_weights, mix.transpose(0, 2, 1), bias.reshape(1, -1), owners.reshape(1, -1))
+    got = pl.pallas_call(
+        copy_kernel,
+        out_shape=jax.ShapeDtypeStruct((np_, 32, 128), BF),
+        in_specs=[any_],
+        out_specs=any_,
+        scratch_shapes=[vm((np_, 32, 128), BF), dma((8,)), dma((8,))],
+        compiler_params=pltpu.CompilerParams(vmem_limit_bytes=62 << 20),
+        name="keep",
+    )(got)
     got = got.reshape(np_, 16, 2, 128).transpose(0, 2, 1, 3).reshape(np_, 2, 2048)
     return got[None]
 

time: 58 us -> 56.6 us (0.976); the launches traced: 57 us -> 56.4 us
  local copies, waits for them, and re-layouts: 2.2 us -> 0 us
  Pallas kernels: 54.8 us -> 56.2 us
    unnamed x1 -> x0, local copies, waits for them, and re-layouts: 2.2 us -> none
    pallas_call x0 -> x1, Pallas kernels: none -> 1.83 us  [body(): pl.pallas_call(copy_kernel, out_shape=jax.ShapeDtypeStruct((np_, 32, 128)...]
where the time goes in v4:
time: 56.6 us; the launch traced here: 56.4 us
  Pallas kernels  56.2 us (99%)
    pallas_call x1, Pallas kernels, body(): pl.pallas_call(functools.partial(cheb_kernel, np_), out_shape=jax.ShapeDt...  54.4 us
    pallas_call x1, Pallas kernels, body(): pl.pallas_call(copy_kernel, out_shape=jax.ShapeDtypeStruct((np_, 32, 128)...  1.83 us

profile of v4, /device:TPU:1, one launch (start us, length us, event | category | flops | bytes accessed | tf_op | source)
XLA Modules:
  0.0 56.4 jit_solution(4508065637966180436)
XLA Ops:
  0.0 54.4 %cheb.1.src = bf16[64,32,128]{2,1,0:T(8,128)(2,1)} custom-call(bf16[32,8192]{1,0:T(8,128)(2,1)} %feat.1, s32[8,8192]{1,0:T(8,128)} %offs.1, f32[8,8192]{1,0:T(8,128)} %wts.1, bf16[8,32,64]{2,1,0:T(8,128)(2,1)} %bitcast.8, f32[1,32]{1,0:T(1,128)} %bitcast.9, s32[1,32]{1,0:T(1,128)} %bitcast.10), custom_call_target="tpu_custom_call" | custom-call | tf_op jit(solution)/shard_map/cheb/pallas_call | solution.py:531
  54.4 1.8 %keep.1 = bf16[64,32,128]{2,1,0:T(8,128)(2,1)} custom-call(bf16[64,32,128]{2,1,0:T(8,128)(2,1)} %cheb.1.src), custom_call_target="tpu_custom_call" | custom-call | tf_op jit(solution)/shard_map/keep/pallas_call | solution.py:551
